TPU v7x, 256 devices: a whole 4x4x8 slice. The times are simulated.
256 devices in a mesh: leaf: 32 (over z, x), blk: 8 (over y, core).
Axes of the slice: x: 4, y: 4, z: 8, core: 2. Of those that a mesh axis runs over, the one named last changes fastest.
Arguments:
- rhs: float32 [6, 32, 4096], P(None, None, ('leaf', 'blk')), may hold values from -6 to 6
- diag_inverse: float32 [4096, 8064], P(('leaf', 'blk')), as said below
- off_diagonal: float32 [5, 4096, 512], P(None, ('leaf', 'blk')), may hold values from -0.1875 to 0.1875
- rows_index: int32 [5, 256, 512], P(None, ('leaf', 'blk')), may hold values from 0 to 7935, as said below
Outputs:
- solution: float32 [6, 32, 4096], P(None, None, ('leaf', 'blk'))
Inputs may be any that keep to these rules, and one draw needn't show every extreme that they name: `diag_inverse`: each level's packed block is lower triangular with a positive diagonal; entries to the right of a supernode's width within its level are zero. `rows_index`: an entry of level l lies below (2**6 - 2**(l+1)) * 128.
All inputs are finite; a program needn't handle non-finite values.
Results may differ from a plain program's by a relative error of at most 0.00013.
Values sent between devices are 32-bit elements; how exact they have to be, the bound alone decides.
No kernel may reach another device: no remote copies, remote signals or barrier semaphores. Data moves between devices by JAX's collectives and lax.ppermute only.
A program may use at most 64 MiB of HBM per device.

v0:
```python
import functools

import jax
import jax.numpy as jnp
from jax import lax
from jax.experimental import pallas as pl
from jax.experimental.pallas import tpu as pltpu
from jax.sharding import Mesh
from jax.sharding import PartitionSpec as P

PLANE = ("x", "blk")
LANES = 128
BLOCK = 16
BLOCKS = 32
ROWS = BLOCK * BLOCKS
REACH = 512
SLOTS = 8
OWN = SLOTS * BLOCK
SPECIES = 4
FIRST = (0, 8, 12, 16, 24, 40)
COUNT = (4, 4, 4, 8, 16, 32)
SPACE = 72
PATH = 64
PARTS = (10, 10, 10, 8, 8)
RHS_AT = 0
NAMED_AT = 256
DIAG_AT = (512, 1152, 1920, 2944, 4480)
OFF_AT = (640, 1408, 2432, 3968, 6528)
CUT = 2944
GROUP = 7040
LEVEL_AT = ((0, 1152), (1152, 1920), (1920, 2944), (2944, 4480), (4480, 7040))
PLANE_DIAG_AT = (0, 128, 384, 896, 1920, 3968)
PLANE_OFF_AT = (8064, 8576, 9088, 9600, 10112)
PLANE_NAMED_AT = 10624
WHOLE = 10880
MIB = 1024 * 1024


def store_named(rows_index, to, at):
    for level in range(5):
        for k in range(2):
            named = rows_index[level, :, k * 256 : (k + 1) * 256].astype(jnp.float32)
            to[2 * level + k : 2 * level + k + 1, at : at + 256] = named
    to[10:16, at : at + 256] = jnp.zeros((6, 256), jnp.float32)


def start_all(moves, sems):
    copies = [pltpu.make_async_copy(source, target, sems.at[k]) for k, (source, target) in enumerate(moves)]
    for copy in copies:
        copy.start()
    return copies


def pack_all(rhs, rows_index, diag_inverse, off_diagonal, pack, first, second, sems):
    moves = []
    for level in range(5):
        part, less = (first, 0) if level < 3 else (second, CUT)
        columns = 2**level * LANES
        diag_at, off_at = DIAG_AT[level] - less, OFF_AT[level] - less
        diag = diag_inverse.at[:, columns - LANES : 2 * columns - LANES]
        moves.append((diag, part.at[:, diag_at : diag_at + columns]))
        moves.append((off_diagonal.at[level], part.at[:, off_at : off_at + REACH]))
    moves.append((diag_inverse, pack.at[:, 0:8064]))
    for level in range(5):
        at = PLANE_OFF_AT[level]
        moves.append((off_diagonal.at[level], pack.at[:, at : at + REACH]))
    copies = start_all(moves, sems)
    given = [rhs[level] for level in range(6)] + [jnp.zeros((BLOCK, 64), jnp.float32)]
    first[:, RHS_AT : RHS_AT + 256] = jnp.concatenate(given, axis=1)
    store_named(rows_index, first, NAMED_AT)
    store_named(rows_index, pack, PLANE_NAMED_AT)
    for copy in copies:
        copy.wait()


def matvec(diag, at, groups, chunks, read_row, write, rows=ROWS):
    size = rows // groups

    def step(k, start):
        total = None
        for c in range(chunks):
            term = diag[pl.ds(start, 64), at + c * LANES : at + (c + 1) * LANES] * read_row(k * chunks + c)
            total = term if total is None else total + term
        write(start, jnp.sum(total, axis=1, keepdims=True))

    for k in range(groups):
        for start in range(k * size, (k + 1) * size, 64):
            step(k, start)


def matvec_transposed(diag, at, groups, chunks, wide, write, rows=ROWS):
    size = rows // groups

    def step(k, c):
        total = None
        for start in range(k * size, (k + 1) * size, 64):
            columns = pl.ds(at + c * LANES, LANES) if isinstance(c, int) else pl.ds(pl.multiple_of(at + c * LANES, LANES), LANES)
            term = diag[start : start + 64, columns] * wide[start : start + 64, :]
            total = term if total is None else total + term
        write(k * chunks + c, jnp.sum(total, axis=0, keepdims=True))

    for k in range(groups):
        for c in range(chunks):
            step(k, c)


def split(value):
    coarse = value.astype(jnp.bfloat16)
    return coarse, (value - coarse.astype(jnp.float32)).astype(jnp.bfloat16)


def rows_iota(rows, first):
    return lax.broadcasted_iota(jnp.int32, (rows, REACH), 0) + first


def small(whole):
    return whole.astype(jnp.float32).astype(jnp.bfloat16)


def pick(hit, value):
    return jnp.where(hit, value, jnp.zeros((), jnp.bfloat16))


def lane_one_hot(where, lanes):
    return pick(lanes == small(jnp.bitwise_and(where, 127)), jnp.ones((), jnp.bfloat16))


def block_rows(d):
    return pl.ds(pl.multiple_of(d * BLOCK, BLOCK), BLOCK)


def couple(off, at, chain, place, first, wide):
    height = SPACE - first
    table = jnp.concatenate(split(chain[first:SPACE, :]), axis=0)
    names, lanes = rows_iota(height, first), small(rows_iota(LANES, 0))

    def step(d, carry):
        where = place[pl.ds(d, 1), :]
        rows = jnp.dot(table, lane_one_hot(where, lanes), preferred_element_type=jnp.float32)
        hit = names == jnp.right_shift(where, 7)
        known = jnp.sum(jnp.where(hit, rows[:height] + rows[height:], 0.0), axis=0, keepdims=True)
        drop = jnp.sum(off[block_rows(d), at : at + REACH] * known, axis=1, keepdims=True)
        wide[block_rows(d), :] = jnp.broadcast_to(-drop, (BLOCK, LANES))
        return carry

    lax.fori_loop(0, BLOCKS, step, 0, unroll=16)


def fetch(pack, held, sems, cuts):
    copies = []
    for k, (first, last, to) in enumerate(cuts):
        copies.append(
            pltpu.make_async_copy(pack.at[:, first:last], held.at[:, to : to + last - first], sems.at[k])
        )
        copies[-1].start()
    return copies


def fetch_named(pack, named, sems, at):
    first = PLANE_NAMED_AT
    copies = [
        pltpu.make_async_copy(pack.at[:, first + k * LANES : first + (k + 1) * LANES], named.at[k], sems.at[at + k])
        for k in range(2)
    ]
    for copy in copies:
        copy.start()
    return copies


def chain_position(named, level, blocks):
    quarters = [
        named.at[a][pl.ds(2 * level + k, blocks, stride=BLOCK), :] for k in range(2) for a in range(2)
    ]
    return jnp.concatenate(quarters, axis=1).astype(jnp.int32) + (2 ** (level + 1) - 1) * LANES


def find_places(named, level, places):
    chain = chain_position(named, level, BLOCKS)
    if level == 0:
        block = lax.broadcasted_iota(jnp.int32, (BLOCKS, REACH), 0)
        places[...] = chain + jnp.where((chain < 3 * LANES) & (block < 16), 7 * LANES, 9 * LANES)
    else:
        places[...] = chain + 9 * LANES


def fetch_parts(parts, level, held, sems):
    first, last = LEVEL_AT[level]
    less = 0 if level < 3 else CUT
    copies, at = [], 0
    for k, part in enumerate(parts):
        count = part.shape[0]
        copies.append(
            pltpu.make_async_copy(part.at[:, first - less : last - less], held.at[pl.ds(at, count), :], sems.at[k])
        )
        copies[-1].start()
        at += count
    return copies


def path_solve(level, read, held, place, wide, total):
    diag_at, off_at = DIAG_AT[level] - LEVEL_AT[level][0], OFF_AT[level] - LEVEL_AT[level][0]
    for n in range(SPECIES):

        def write(at, value, n=n):
            wide[n, at : at + 64, :] = jnp.broadcast_to(value, (64, LANES))

        matvec(held, diag_at, 1, 2**level, functools.partial(read, n), write, OWN)
    names, lanes = small(rows_iota(PATH, 0)), small(rows_iota(LANES, 0))
    total[...] = jnp.zeros_like(total)

    def slot(d, carry):
        where = place[pl.ds(d, 1), :]
        hit = names == small(jnp.right_shift(where, 7))
        right = lane_one_hot(where, lanes)
        rows = block_rows(d)
        left = []
        for n in range(SPECIES):
            solved = jnp.concatenate([wide[n, rows, :]] * (REACH // LANES), axis=1)
            update = jnp.sum(held[rows, off_at : off_at + REACH] * solved, axis=0, keepdims=True)
            left += [pick(hit, part) for part in split(update)]
        total[...] += lax.dot_general(
            jnp.concatenate(left, axis=0), right, (((1,), (1,)), ((), ())), preferred_element_type=jnp.float32
        )
        return carry

    lax.fori_loop(0, SLOTS, slot, 0, unroll=4)


def path_update(level, before, total, path, ahead):
    count = 2 ** (level + 1)
    for n in range(SPECIES):
        at = 2 * n * PATH
        path[n * PATH : (n + 1) * PATH, :] = before[n * PATH : (n + 1) * PATH, :] - (
            total[at : at + PATH, :] + total[at + PATH : at + 2 * PATH, :]
        )
        if ahead is not None:
            ahead[n * count : (n + 1) * count, :] = path[n * PATH + count : n * PATH + 2 * count, :]


def path_first(*refs):
    parts = refs[: PARTS[0]]
    here, path, ahead, r0, places, held, named, turned, wide, total, sems = refs[PARTS[0] :]
    leaf, b = here[0], here[1]
    copies = fetch_parts(parts, 0, held, sems)
    path[...] = jnp.zeros((SPECIES * PATH, LANES), jnp.float32)
    lane = lax.broadcasted_iota(jnp.int32, (BLOCK, LANES), 1)
    row = lax.broadcasted_iota(jnp.int32, (BLOCK, LANES), 0)
    stands = []
    for core in (0, 1):
        for ahead_by in (0, 6, 2, 4):
            slot = jnp.bitwise_and(b + ahead_by, 7) ^ core
            stands.append(jnp.where(lane == row + slot * BLOCK, 1.0, 0.0).astype(jnp.bfloat16))
    order = jnp.concatenate(stands, axis=0)
    for copy in copies:
        copy.wait()
    flipped = jnp.transpose(held[:, RHS_AT : RHS_AT + 256])
    total_rows = None
    for _ in range(3):
        piece = flipped.astype(jnp.bfloat16)
        flipped = flipped - piece.astype(jnp.float32)
        rows = jnp.dot(piece, order, preferred_element_type=jnp.float32)
        total_rows = rows if total_rows is None else total_rows + rows
    turned[...] = total_rows
    for n in range(SPECIES):
        r0[n : n + 1, :] = turned[pl.ds(b * SPECIES + n, 1), :]
        for level in range(1, 6):
            at = n * PATH + 2**level + jnp.bitwise_and(leaf, 2**level - 1)
            path[pl.ds(at, 1), :] = turned[pl.ds(level * 32 + b * SPECIES + n, 1), :]
    for k in range(2):
        named[k] = held[:, NAMED_AT + k * LANES : NAMED_AT + (k + 1) * LANES]
    for level in range(5):
        places[level] = chain_position(named, level, SLOTS) + LANES
    path_solve(0, lambda n, c: r0[n : n + 1, :], held, places.at[0], wide, total)
    path_update(0, path, total, path, ahead)


def path_next(level, *refs):
    parts = refs[: PARTS[level]]
    places, summed, before, path, ahead, held, wide, total, sems = refs[PARTS[level] :]
    copies = fetch_parts(parts, level, held, sems)
    count = 2**level
    for copy in copies:
        copy.wait()
    path_solve(
        level, lambda n, c: summed[n * count + c : n * count + c + 1, :], held, places.at[level], wide, total
    )
    path_update(level, before, total, path, ahead)


def path_last(*refs):
    parts, (place, places, r0, r1, r2, r3, summed, before, keep, send, t2, t3, t4, path, *scratch) = (
        refs[: PARTS[4]], refs[PARTS[4] :]
    )
    path_next(4, *parts, places, summed, before, path, None, *scratch)
    x = place[0]
    even = 1.0 - (x & 1).astype(jnp.float32)
    for n in range(SPECIES):
        slot = n ^ x
        slot = slot ^ (slot >> 1)
        value = jnp.zeros((8, LANES), jnp.float32)
        row = lax.broadcasted_iota(jnp.int32, (8, LANES), 0)
        value = jnp.where(row == x, r0[n : n + 1, :], value)
        for k in range(2):
            value = jnp.where(row == 4 + 2 * (x >> 1) + k, r1[2 * n + k : 2 * n + k + 1, :] * even, value)
        for to, low in ((keep, 0), (send, 2)):

            @pl.when((slot >= low) & (slot < low + 2))
            def _(n=n, slot=slot, value=value, to=to, low=low):
                to[slot - low, 0:32, :] = path[n * PATH + 32 : (n + 1) * PATH, :]
                to[slot - low, 32:40, :] = value

    t2[...] = r2[pl.ds(x * 4, 4), :]
    t3[...] = r3[pl.ds(pl.multiple_of(x * 8, 8), 8), :]
    t4[...] = summed[pl.ds(pl.multiple_of(x * 16, 16), 16), :]


def high_cuts(level):
    columns = COUNT[level] * LANES
    return [
        (PLANE_DIAG_AT[level], PLANE_DIAG_AT[level] + columns, 0),
        (PLANE_OFF_AT[level], PLANE_OFF_AT[level] + REACH, columns),
    ]


def top(pack, summed, partial, held, wide, sems):
    pieces = 8
    size = ROWS // pieces

    def piece(k):
        rows = pl.ds(pl.multiple_of(k * size, size), size)
        columns = pl.ds(PLANE_DIAG_AT[5], COUNT[5] * LANES)
        return rows, pltpu.make_async_copy(pack.at[rows, columns], held.at[rows, :], sems.at[k])

    for k in range(pieces):
        piece(k)[1].start()
    partial[...] = jnp.zeros((COUNT[5], LANES), jnp.float32)

    @pl.loop(0, pieces)
    def _(k):
        rows, copy = piece(k)
        copy.wait()

        def write(at, value):
            wide[...] = jnp.broadcast_to(value, (size, LANES))

        matvec(held.at[rows, :], 0, 1, COUNT[5], lambda c: summed[c : c + 1, :], write, size)

        def write_row(c, value):
            partial[pl.ds(c, 1), :] = partial[pl.ds(c, 1), :] + value

        for c in range(COUNT[5]):
            term = held[rows, c * LANES : (c + 1) * LANES] * wide[...]
            write_row(c, jnp.sum(term, axis=0, keepdims=True))


def backward_high(level, pack, residual, *rest):
    above = rest[: 5 - level]
    partial, held, wide, chain, named, places, sems = rest[5 - level :]
    columns = COUNT[level] * LANES
    named_copies = fetch_named(pack, named, sems, 6)
    copies = fetch(pack, held, sems, high_cuts(level)[::-1])
    for k, value in enumerate(above):
        chain[FIRST[5 - k] : FIRST[5 - k] + COUNT[5 - k], :] = value[...]
    for copy in named_copies:
        copy.wait()
    find_places(named, level, places)
    copies[0].wait()
    couple(held, columns, chain, places, FIRST[level + 1], wide)
    copies[1].wait()

    def write(at, value):
        wide[pl.ds(at, 64), :] = wide[pl.ds(at, 64), :] + value

    matvec(held, 0, 1, COUNT[level], lambda c: residual[c : c + 1, :], write)

    def write_row(c, value):
        partial[pl.ds(c, 1), :] = value

    matvec_transposed(held, 0, 1, COUNT[level], wide, write_row)


def backward_low(pack, r01, r2, s5, s4, s3, out, held, wide, chain, named, places, sems):
    named_copies = fetch_named(pack, named, sems, 6)
    cuts = []
    for level in (2, 1, 0):
        diag_at, off_at = PLANE_DIAG_AT[level], PLANE_OFF_AT[level]
        cuts.append((off_at, off_at + REACH, 896 + REACH * level))
        cuts.append((diag_at, diag_at + LANES * 2**level, LANES * (2**level - 1)))
    copies = fetch(pack, held, sems, cuts)
    for level, value in ((5, s5), (4, s4), (3, s3)):
        chain[FIRST[level] : FIRST[level] + COUNT[level], :] = value[...]
    chain[0:16, :] = jnp.zeros((16, LANES), jnp.float32)
    for copy in named_copies:
        copy.wait()
    for k, level in enumerate((2, 1, 0)):
        find_places(named, level, places)
        copies[2 * k].wait()
        couple(held, 896 + REACH * level, chain, places, 8, wide)

        def write(at, value):
            wide[pl.ds(at, 64), :] = wide[pl.ds(at, 64), :] + value

        def read(c, level=level):
            return r2[c : c + 1, :] if level == 2 else r01[4 * level + c : 4 * level + c + 1, :]

        copies[2 * k + 1].wait()
        matvec(held, LANES * (2**level - 1), 4 >> level, 1 << level, read, write)

        def write_row(c, value, first=FIRST[level]):
            chain[first + c : first + c + 1, :] = value

        matvec_transposed(held, LANES * (2**level - 1), 4 >> level, 1 << level, wide, write_row)
    out[...] = chain[0:16, :]


def call(body, outs, scratch, args, far=1, scalar=(), sems=8):
    vmem = pl.BlockSpec(memory_space=pltpu.VMEM)
    smem = pl.BlockSpec(memory_space=pltpu.SMEM)
    hbm = pl.BlockSpec(memory_space=pltpu.HBM)
    specs = [hbm if k < far else smem if k in scalar else vmem for k in range(len(args))]
    return pl.pallas_call(
        body,
        out_shape=outs,
        in_specs=specs,
        out_specs=jax.tree.map(lambda _: vmem, outs),
        scratch_shapes=scratch + [pltpu.SemaphoreType.DMA((sems,))],
        compiler_params=pltpu.CompilerParams(vmem_limit_bytes=(52 if far == 1 else 6) * MIB),
        cost_estimate=pl.CostEstimate(flops=2**29, bytes_accessed=2**20, transcendentals=0),
    )(*args)


def shape(*dims, kind=jnp.float32):
    return jax.ShapeDtypeStruct(dims, kind)


def moved(value, axis, to):
    size = lax.axis_size(axis)
    return lax.ppermute(value, axis, [(i, to(i)) for i in range(size)])


def near_x(i):
    return 3 - i


def far_z(i):
    return (i + 5) % 8 if i % 2 else (i + 3) % 8


def sum_leaf(value, first, last):
    steps = [("x", lambda i: i ^ 1), ("x", near_x), ("z", lambda i: i ^ 1)]
    if last < 5:
        steps.append(("z", lambda i: i ^ 2))
    else:
        steps.append(("z", lambda i: (i + 1) % 8 if i % 2 else (i + 7) % 8))
        steps.append(("z", far_z))
    for axis, to in steps[first:last]:
        value = value + moved(value, axis, to)
    return value


def local(rhs, diag_inverse, off_diagonal, rows_index):
    f32 = jnp.float32
    x, z = lax.axis_index("x"), lax.axis_index("z")
    leaf = z * 4 + x
    hbm, vmem = pl.BlockSpec(memory_space=pltpu.HBM), pl.BlockSpec(memory_space=pltpu.VMEM)
    pack, first, second = pl.pallas_call(
        pack_all,
        out_shape=(shape(BLOCK, WHOLE), shape(BLOCK, CUT), shape(BLOCK, GROUP - CUT)),
        in_specs=[vmem, vmem, hbm, hbm],
        out_specs=(vmem,) * 3,
        scratch_shapes=[pltpu.SemaphoreType.DMA((16,))],
        compiler_params=pltpu.CompilerParams(vmem_limit_bytes=6 * MIB),
    )(jnp.transpose(rhs, (0, 2, 1)), rows_index, diag_inverse, off_diagonal)
    pack = lax.all_gather(pack, PLANE, axis=0, tiled=True)

    def other_core(parts):
        return parts + tuple(moved(part, "blk", lambda i: i ^ 1) for part in parts)

    half = BLOCK // 2
    down, up = (moved(first, "blk", lambda i, hop=hop: (i + hop) % SLOTS) for hop in (2, 6))
    across = (
        moved(down[:half], "blk", lambda i: (i + 2) % SLOTS),
        moved(up[half:], "blk", lambda i: (i + 6) % SLOTS),
    )
    first = other_core((first, down, up, *across))
    second = lax.optimization_barrier((second, first[-1]))[0]
    second = (second,) + tuple(moved(second, "blk", lambda i, hop=hop: (i + hop) % SLOTS) for hop in (2, 6, 4))

    def path_scratch(level, *more):
        return [
            pltpu.VMEM((OWN, LEVEL_AT[level][1] - LEVEL_AT[level][0]), f32),
            *more,
            pltpu.VMEM((SPECIES, OWN, LANES), f32),
            pltpu.VMEM((SPECIES * 2 * PATH, LANES), f32),
        ]

    here = jnp.stack([leaf, lax.axis_index("blk")]).astype(jnp.int32)
    path, ahead, r0, places = call(
        path_first,
        (
            shape(SPECIES * PATH, LANES), shape(SPECIES * 2, LANES), shape(SPECIES, LANES),
            shape(5, SLOTS, REACH, kind=jnp.int32),
        ),
        path_scratch(0, pltpu.VMEM((2, OWN, LANES), f32), pltpu.VMEM((256, LANES), f32)),
        (*first, here),
        far=PARTS[0],
        scalar=(PARTS[0],),
        sems=PARTS[0],
    )
    waiting = [r0, sum_leaf(ahead, 0, 1)]
    for level in (1, 2, 3):
        path, ahead = call(
            functools.partial(path_next, level),
            (shape(SPECIES * PATH, LANES), shape(SPECIES * 2 ** (level + 1), LANES)),
            path_scratch(level),
            (*(first if level < 3 else second), places, waiting[level], path),
            far=PARTS[level],
            sems=PARTS[level],
        )
        if level == 2:
            second = other_core(lax.optimization_barrier((*second, ahead))[:4])
        waiting.append(sum_leaf(ahead, 0, level + 1))
    keep, send, r2, r3, r4 = call(
        path_last,
        (shape(2, 40, LANES), shape(2, 40, LANES), shape(4, LANES), shape(8, LANES), shape(16, LANES)),
        [pltpu.VMEM((SPECIES * PATH, LANES), f32)] + path_scratch(4),
        (*second, x.astype(jnp.int32).reshape(1), places, *waiting, path),
        far=PARTS[4],
        scalar=(PARTS[4],),
        sems=PARTS[4],
    )
    keep = keep + moved(send, "x", near_x)
    turned = keep[0] + moved(keep[1], "x", lambda i: i ^ 1)
    r5 = sum_leaf(turned[0:32], 2, 5)

    wide, chain = pltpu.VMEM((ROWS, LANES), f32), pltpu.VMEM((SPACE, LANES), f32)
    named, places = pltpu.VMEM((2, ROWS, LANES), f32), pltpu.VMEM((BLOCKS, REACH), jnp.int32)
    partial = call(top, shape(32, LANES), [pltpu.VMEM((ROWS, 32 * LANES), f32), pltpu.VMEM((ROWS // 8, LANES), f32)], (pack, r5))
    known = [sum_leaf(partial, 2, 5)]
    for level, from_rows in ((4, r4), (3, r3)):
        count = COUNT[level]
        partial = call(
            functools.partial(backward_high, level),
            shape(count, LANES),
            [pltpu.VMEM((ROWS, count * LANES + REACH), f32), wide, chain, named, places],
            (pack, from_rows, *known),
        )
        known.append(sum_leaf(partial, 2, level))
    last = call(
        backward_low,
        shape(16, LANES),
        [pltpu.VMEM((ROWS, 896 + 3 * REACH), f32), wide, chain, named, places],
        (pack, turned[32:40], r2, *known),
    )
    pieces = [last[0:4], last[8:12], last[12:16]]
    for level in (3, 4, 5):
        place = jnp.remainder(z, 2 ** (level - 2)) * 4
        pieces.append(lax.dynamic_slice_in_dim(known[5 - level], place, 4, 0))
    out = jnp.stack(pieces).reshape(6, BLOCKS, BLOCK)
    out = lax.all_to_all(jnp.transpose(out, (1, 0, 2)), PLANE, 0, 0)
    return jnp.transpose(out.reshape(SPECIES, SLOTS, 6, BLOCK), (2, 1, 0, 3)).reshape(6, BLOCKS, BLOCK)


def solution(mesh):
    cut = Mesh(mesh.devices.reshape(8, 4, 8), ("z", "x", "blk"))
    rows = ("z", "x", "blk")
    placed = (P(None, None, rows), P(rows, None), P(None, rows, None), P(None, rows, None))
    return jax.shard_map(
        local, mesh=cut, in_specs=placed, out_specs=P(None, None, rows), check_vma=False
    )
```

profile of v0, /device:TPU:1, one launch (start us, length us, event | category | flops | bytes accessed | tf_op | source)
XLA Modules:
  0.0 185.6 jit_solution(14996587520565648500)
XLA Ops:
  10.0 1.6 shard_map.46
  11.7 3.6 %collective-permute-start = (f32[16,2944]{1,0:T(8,128)S(1)}, f32[16,2944]{1,0:T(8,128)S(1)}, u32[]{:S(2)}, u32[]{:S(2)}) collective-permute-start(f32[16,2944]{1,0:T(8,128)S(1)} %get-tuple-element.30.refs_0_), channel_id=1, source_target_pairs={{0,6},{1,7},{2,0},{3,1},{4,2},{5,3},{6,4},{7,5},{8,14},{9,15},{10,... | collective-permute-start | bytes 565256 | tf_op jit(solution)/shard_map/ppermute | solution.py:438
  15.3 3.4 %collective-permute-done.refs_2_ = f32[16,2944]{1,0:T(8,128)S(1)} collective-permute-done((f32[16,2944]{1,0:T(8,128)S(1)}, f32[16,2944]{1,0:T(8,128)S(1)}, u32[]{:S(2)}, u32[]{:S(2)}) %collective-permute-start) | collective-permute-done | bytes 188448 | tf_op jit(solution)/shard_map/ppermute | solution.py:438
  18.7 3.5 %collective-permute-start.1 = (f32[8,2944]{1,0:T(8,128)S(1)}, f32[8,2944]{1,0:T(8,128)S(1)}, u32[]{:S(2)}, u32[]{:S(2)}) collective-permute-start(f32[8,2944]{1,0:T(8,128)S(1)} %slice.36), channel_id=1, source_target_pairs={{0,6},{1,7},{2,0},{3,1},{4,2},{5,3},{6,4},{7,5},{8,14},{9,15},{10,... | collective-permute-start | bytes 282632 | tf_op jit(solution)/shard_map/ppermute | solution.py:438
  22.2 1.8 collective-permute-start.8
  24.1 2.1 %collective-permute-start.2 = (f32[8,2944]{1,0:T(8,128)S(1)}, f32[8,2944]{1,0:T(8,128)S(1)}, u32[]{:S(2)}, u32[]{:S(2)}) collective-permute-start(f32[8,2944]{1,0:T(8,128)S(1)} %collective-permute-done.1.refs_4_), channel_id=1, source_target_pairs={{0,1},{1,0},{2,3},{3,2},{4,5},{5,4},{6,7},{7,6},{8,9},{9,8},{10,11... | collective-permute-start | bytes 282632 | tf_op jit(solution)/shard_map/ppermute | solution.py:438
  26.2 3.5 %collective-permute-done.7.refs_3_ = f32[8,2944]{1,0:T(8,128)S(1)} collective-permute-done((f32[8,2944]{1,0:T(8,128)S(1)}, f32[8,2944]{1,0:T(8,128)S(1)}, u32[]{:S(2)}, u32[]{:S(2)}) %collective-permute-start.7) | collective-permute-done | bytes 94240 | tf_op jit(solution)/shard_map/ppermute | solution.py:438
  31.0 2.7 %collective-permute-start.4 = (f32[16,4096]{1,0:T(8,128)S(1)}, f32[16,4096]{1,0:T(8,128)S(1)}, u32[]{:S(2)}, u32[]{:S(2)}) collective-permute-start(f32[16,4096]{1,0:T(8,128)S(1)} %get-tuple-element.38.refs_0_), channel_id=1, source_target_pairs={{0,6},{1,7},{2,0},{3,1},{4,2},{5,3},{6,4},{7,5},{8,14},{9,15},{10,... | collective-permute-start | bytes 786440 | tf_op jit(solution)/shard_map/ppermute | solution.py:438
  33.7 3.0 %shard_map.47 = (f32[256,128]{1,0:T(8,128)S(1)}, f32[8,128]{1,0:T(8,128)S(1)}, f32[4,128]{1,0:T(4,128)S(1)}, s32[5,8,512]{2,1,0:T(8,128)S(1)}) custom-call(f32[16,2944]{1,0:T(8,128)S(1)} %get-tuple-element.30.refs_0_, f32[16,2944]{1,0:T(8,128)S(1)} %collective-permute-done.6.refs_1_, f32[16,2944]{1,0:T(8,128)S(1)} %collective-permute-done.refs_2_, ...), custom_call_target="tpu_custom_call" | custom-call | flops 536870912 | bytes 1048576 | tf_op jit(solution)/shard_map/pallas_call | solution.py:421
  38.1 1.6 collective-permute-done.12
  39.7 2.0 %shard_map.48 = (f32[256,128]{1,0:T(8,128)S(1)}, f32[16,128]{1,0:T(8,128)S(1)}) custom-call(f32[16,2944]{1,0:T(8,128)S(1)} %get-tuple-element.30.refs_0_, f32[16,2944]{1,0:T(8,128)S(1)} %collective-permute-done.6.refs_1_, f32[16,2944]{1,0:T(8,128)S(1)} %collective-permute-done.refs_2_, f32[8,2944]{1,0:T(8,128)S(1)} %collective-permute-done.7.refs_3_, ...), custom_call_target="tpu_custom_call" | custom-call | flops 536870912 | bytes 1048576 | tf_op jit(solution)/shard_map/pallas_call | solution.py:421
  43.0 1.7 collective-permute-done.13
  44.7 2.5 %collective-permute-start.14 = (f32[16,128]{1,0:T(8,128)S(1)}, f32[16,128]{1,0:T(8,128)S(1)}, u32[]{:S(2)}, u32[]{:S(2)}) collective-permute-start(f32[16,128]{1,0:T(8,128)S(1)} %add.87), channel_id=1, source_target_pairs={{0,24},{8,16},{16,8},{24,0},{1,25},{9,17},{17,9},{25,1},{2,26},{10... | collective-permute-start | bytes 24584 | tf_op jit(solution)/shard_map/ppermute | solution.py:438
  47.2 1.6 collective-permute-done.14
  48.9 2.1 %shard_map.49 = (f32[256,128]{1,0:T(8,128)S(1)}, f32[32,128]{1,0:T(8,128)S(1)}) custom-call(f32[16,2944]{1,0:T(8,128)S(1)} %get-tuple-element.30.refs_0_, f32[16,2944]{1,0:T(8,128)S(1)} %collective-permute-done.6.refs_1_, f32[16,2944]{1,0:T(8,128)S(1)} %collective-permute-done.refs_2_, f32[8,2944]{1,0:T(8,128)S(1)} %collective-permute-done.7.refs_3_, ...), custom_call_target="tpu_custom_call" | custom-call | flops 536870912 | bytes 1048576 | tf_op jit(solution)/shard_map/pallas_call | solution.py:421
  51.0 3.5 %collective-permute-done.5.refs_3_ = f32[16,4096]{1,0:T(8,128)S(1)} collective-permute-done((f32[16,4096]{1,0:T(8,128)S(1)}, f32[16,4096]{1,0:T(8,128)S(1)}, u32[]{:S(2)}, u32[]{:S(2)}) %collective-permute-start.5) | collective-permute-done | bytes 262176 | tf_op jit(solution)/shard_map/ppermute | solution.py:438
  58.8 2.5 %collective-permute-start.20 = (f32[32,128]{1,0:T(8,128)S(1)}, f32[32,128]{1,0:T(8,128)S(1)}, u32[]{:S(2)}, u32[]{:S(2)}) collective-permute-start(f32[32,128]{1,0:T(8,128)S(1)} %add.89), channel_id=1, source_target_pairs={{0,24},{8,16},{16,8},{24,0},{1,25},{9,17},{17,9},{25,1},{2,26},{10... | collective-permute-start | bytes 49160 | tf_op jit(solution)/shard_map/ppermute | solution.py:438
  62.6 1.5 collective-permute-start.21
  65.3 2.3 %shard_map.50 = (f32[256,128]{1,0:T(8,128)S(1)}, f32[64,128]{1,0:T(8,128)S(1)}) custom-call(f32[16,4096]{1,0:T(8,128)S(1)} %get-tuple-element.38.refs_0_, f32[16,4096]{1,0:T(8,128)S(1)} %collective-permute-done.3.refs_1_, f32[16,4096]{1,0:T(8,128)S(1)} %collective-permute-done.4.refs_2_, f32[16,4096]{1,0:T(8,128)S(1)} %collective-permute-done.5.refs_3_, ...), custom_call_target="tpu_custom_call" | custom-call | flops 536870912 | bytes 1048576 | tf_op jit(solution)/shard_map/pallas_call | solution.py:421
  67.7 3.8 %collective-permute-done.22 = f32[64,128]{1,0:T(8,128)S(1)} collective-permute-done((f32[64,128]{1,0:T(8,128)S(1)}, f32[64,128]{1,0:T(8,128)S(1)}, u32[]{:S(2)}, u32[]{:S(2)}) %collective-permute-start.22) | collective-permute-done | bytes 32800 | tf_op jit(solution)/shard_map/ppermute | solution.py:438
  71.5 2.5 %collective-permute-start.23 = (f32[64,128]{1,0:T(8,128)S(1)}, f32[64,128]{1,0:T(8,128)S(1)}, u32[]{:S(2)}, u32[]{:S(2)}) collective-permute-start(f32[64,128]{1,0:T(8,128)S(1)} %add.92), channel_id=1, source_target_pairs={{0,24},{8,16},{16,8},{24,0},{1,25},{9,17},{17,9},{25,1},{2,26},{10... | collective-permute-start | bytes 98312 | tf_op jit(solution)/shard_map/ppermute | solution.py:438
  73.9 2.6 %collective-permute-done.23 = f32[64,128]{1,0:T(8,128)S(1)} collective-permute-done((f32[64,128]{1,0:T(8,128)S(1)}, f32[64,128]{1,0:T(8,128)S(1)}, u32[]{:S(2)}, u32[]{:S(2)}) %collective-permute-start.23) | collective-permute-done | bytes 32800 | tf_op jit(solution)/shard_map/ppermute | solution.py:438
  76.5 1.5 collective-permute-start.24
  78.0 1.7 collective-permute-done.24
  79.8 2.5 %collective-permute-start.25 = (f32[64,128]{1,0:T(8,128)S(1)}, f32[64,128]{1,0:T(8,128)S(1)}, u32[]{:S(2)}, u32[]{:S(2)}) collective-permute-start(f32[64,128]{1,0:T(8,128)S(1)} %add.94), channel_id=1, source_target_pairs={{0,64},{32,96},{64,0},{96,32},{128,192},{160,224},{192,128},{224,1... | collective-permute-start | bytes 98312 | tf_op jit(solution)/shard_map/ppermute | solution.py:438
  82.2 1.7 collective-permute-done.25
  83.9 2.9 %shard_map.51 = (f32[2,40,128]{2,1,0:T(8,128)S(1)}, f32[2,40,128]{2,1,0:T(8,128)S(1)}, f32[4,128]{1,0:T(4,128)S(1)}, f32[8,128]{1,0:T(8,128)S(1)}, f32[16,128]{1,0:T(8,128)S(1)}) custom-call(f32[16,4096]{1,0:T(8,128)S(1)} %get-tuple-element.38.refs_0_, f32[16,4096]{1,0:T(8,128)S(1)} %collective-permute-done.3.refs_1_, ...), custom_call_target="tpu_custom_call" | custom-call | flops 536870912 | bytes 1048576 | tf_op jit(solution)/shard_map/pallas_call | solution.py:421
  86.8 2.5 %collective-permute-start.26 = (f32[2,40,128]{2,1,0:T(8,128)S(1)}, f32[2,40,128]{2,1,0:T(8,128)S(1)}, u32[]{:S(2)}, u32[]{:S(2)}) collective-permute-start(f32[2,40,128]{2,1,0:T(8,128)S(1)} %get-tuple-element.47), channel_id=1, source_target_pairs={{0,24},{8,16},{16,8},{24,0},{1,25},{9,17},{17,9},{25,1},{2,26},{10... | collective-permute-start | bytes 122888 | tf_op jit(solution)/shard_map/ppermute | solution.py:438
  89.3 2.9 %collective-permute-done.26 = f32[2,40,128]{2,1,0:T(8,128)S(1)} collective-permute-done((f32[2,40,128]{2,1,0:T(8,128)S(1)}, f32[2,40,128]{2,1,0:T(8,128)S(1)}, u32[]{:S(2)}, u32[]{:S(2)}) %collective-permute-start.26) | collective-permute-done | bytes 40992 | tf_op jit(solution)/shard_map/ppermute | solution.py:438
  92.3 3.4 %collective-permute-done.27 = f32[40,128]{1,0:T(8,128)S(1)} collective-permute-done((f32[40,128]{1,0:T(8,128)S(1)}, f32[40,128]{1,0:T(8,128)S(1)}, u32[]{:S(2)}, u32[]{:S(2)}) %collective-permute-start.27) | collective-permute-done | bytes 20512 | tf_op jit(solution)/shard_map/ppermute | solution.py:438
  97.2 1.6 collective-permute-done.28
  98.8 3.7 %collective-permute-start.29 = (f32[32,128]{1,0:T(8,128)S(1)}, f32[32,128]{1,0:T(8,128)S(1)}, u32[]{:S(2)}, u32[]{:S(2)}) collective-permute-start(f32[32,128]{1,0:T(8,128)S(1)} %slice_add_fusion), channel_id=1, source_target_pairs={{0,224},{32,64},{64,32},{96,128},{128,96},{160,192},{192,160},{224... | collective-permute-start | bytes 49160 | tf_op jit(solution)/shard_map/ppermute | solution.py:438
  102.5 1.5 collective-permute-done.29
  104.1 2.6 %collective-permute-start.30 = (f32[32,128]{1,0:T(8,128)S(1)}, f32[32,128]{1,0:T(8,128)S(1)}, u32[]{:S(2)}, u32[]{:S(2)}) collective-permute-start(f32[32,128]{1,0:T(8,128)S(1)} %add.99), channel_id=1, source_target_pairs={{0,96},{32,192},{64,160},{96,0},{128,224},{160,64},{192,32},{224,1... | collective-permute-start | bytes 49160 | tf_op jit(solution)/shard_map/ppermute | solution.py:438
  106.7 2.0 %collective-permute-done.30 = f32[32,128]{1,0:T(8,128)S(1)} collective-permute-done((f32[32,128]{1,0:T(8,128)S(1)}, f32[32,128]{1,0:T(8,128)S(1)}, u32[]{:S(2)}, u32[]{:S(2)}) %collective-permute-start.30) | collective-permute-done | bytes 16416 | tf_op jit(solution)/shard_map/ppermute | solution.py:438
  108.7 9.5 %all-gather.2.cloned.1.call-done.pack = f32[512,10880]{1,0:T(8,128)} async-done(((f32[16,10880]{1,0:T(8,128)}), f32[512,10880]{1,0:T(8,128)}) %all-gather.2.cloned.1.call-update) | async-done | bytes 22282256 | tf_op jit(solution)/shard_map/all_gather | solution.py:474
  118.2 3.7 %shard_map.52 = f32[32,128]{1,0:T(8,128)S(1)} custom-call(f32[512,10880]{1,0:T(8,128)} %all-gather.2.cloned.1.call-done.pack, f32[32,128]{1,0:T(8,128)S(1)} %add.100.summed), custom_call_target="tpu_custom_call" | custom-call | flops 536870912 | bytes 1048576 | tf_op jit(solution)/shard_map/pallas_call | solution.py:421
  121.9 1.6 collective-permute-start.31
  124.8 3.0 %collective-permute-start.32 = (f32[32,128]{1,0:T(8,128)S(1)}, f32[32,128]{1,0:T(8,128)S(1)}, u32[]{:S(2)}, u32[]{:S(2)}) collective-permute-start(f32[32,128]{1,0:T(8,128)S(1)} %add.101), channel_id=1, source_target_pairs={{0,224},{32,64},{64,32},{96,128},{128,96},{160,192},{192,160},{224... | collective-permute-start | bytes 49160 | tf_op jit(solution)/shard_map/ppermute | solution.py:438
  129.0 2.9 %collective-permute-start.33 = (f32[32,128]{1,0:T(8,128)S(1)}, f32[32,128]{1,0:T(8,128)S(1)}, u32[]{:S(2)}, u32[]{:S(2)}) collective-permute-start(f32[32,128]{1,0:T(8,128)S(1)} %add.102), channel_id=1, source_target_pairs={{0,96},{32,192},{64,160},{96,0},{128,224},{160,64},{192,32},{224,1... | collective-permute-start | bytes 49160 | tf_op jit(solution)/shard_map/ppermute | solution.py:438
  131.9 1.5 collective-permute-done.33
  133.4 3.4 %shard_map.53 = f32[16,128]{1,0:T(8,128)S(1)} custom-call(f32[512,10880]{1,0:T(8,128)} %all-gather.2.cloned.1.call-done.pack, f32[16,128]{1,0:T(8,128)S(1)} %get-tuple-element.49.residual, f32[32,128]{1,0:T(8,128)S(1)} %add.103.rest_0_.s5), custom_call_target="tpu_custom_call" | custom-call | flops 536870912 | bytes 1048576 | tf_op jit(solution)/shard_map/pallas_call | solution.py:421
  137.8 1.6 collective-permute-done.34
  139.4 1.9 %collective-permute-start.35 = (f32[16,128]{1,0:T(8,128)S(1)}, f32[16,128]{1,0:T(8,128)S(1)}, u32[]{:S(2)}, u32[]{:S(2)}) collective-permute-start(f32[16,128]{1,0:T(8,128)S(1)} %add.104), channel_id=1, source_target_pairs={{0,64},{32,96},{64,0},{96,32},{128,192},{160,224},{192,128},{224,1... | collective-permute-start | bytes 24584 | tf_op jit(solution)/shard_map/ppermute | solution.py:438
  142.8 3.1 %shard_map.54 = f32[8,128]{1,0:T(8,128)S(1)} custom-call(f32[512,10880]{1,0:T(8,128)} %all-gather.2.cloned.1.call-done.pack, f32[8,128]{1,0:T(8,128)S(1)} %get-tuple-element.50.residual, f32[32,128]{1,0:T(8,128)S(1)} %add.103.rest_0_.s5, f32[16,128]{1,0:T(8,128)S(1)} %add.105.rest_1_.s4), custom_call_target="tpu_custom_call" | custom-call | flops 536870912 | bytes 1048576 | tf_op jit(solution)/shard_map/pallas_call | solution.py:421
  147.0 1.8 collective-permute-done.36
  148.8 6.8 %shard_map.55 = f32[16,128]{1,0:T(8,128)S(1)} custom-call(f32[512,10880]{1,0:T(8,128)} %all-gather.2.cloned.1.call-done.pack, f32[8,128]{1,0:T(8,128)S(1)} %slice.40.r01, f32[4,128]{1,0:T(4,128)S(1)} %get-tuple-element.48.r2, f32[32,128]{1,0:T(8,128)S(1)} %add.103.rest_0_.s5, f32[16,128]{1,0:T(8,128)S(1)} %add.105.rest_1_.s4, f32[8,128]{1,0:T(8,128)S(1)} %add.106.s3), custom_call_target="tpu_custom_call" | custom-call | flops 536870912 | bytes 1048576 | tf_op jit(solution)/shard_map/pallas_call | solution.py:421
  156.1 21.9 %all_to_all.5 = f32[32,6,16]{2,1,0:T(8,128)S(1)} all-to-all(f32[32,6,16]{2,1,0:T(8,128)S(1)} %copy.8), channel_id=1, replica_groups=mesh['z'=8,'x'=4,'blk'=8] {'x','blk'}, dimensions={0} | all-to-all | bytes 24576 | tf_op jit(solution)/shard_map/all_to_all | solution.py:560
  (94 shorter events, 23.3 us)
Async XLA Ops:
  6.5 111.7 %all-gather.2.cloned.1.call-start = ((), (), s32[]{:S(2)}) async-start(), calls=%async_computation.1 | async-start | bytes 22978560 | tf_op jit(solution)/shard_map/all_gather | solution.py:474
  6.5 1.0 copy-start
  7.6 0.9 copy-start.1
  8.5 0.8 copy-start.2
  9.3 0.7 copy-start.3
  11.7 7.0 %collective-permute-start = (f32[16,2944]{1,0:T(8,128)S(1)}, f32[16,2944]{1,0:T(8,128)S(1)}, u32[]{:S(2)}, u32[]{:S(2)}) collective-permute-start(f32[16,2944]{1,0:T(8,128)S(1)} %get-tuple-element.30.refs_0_), channel_id=1, source_target_pairs={{0,6},{1,7},{2,0},{3,1},{4,2},{5,3},{6,4},{7,5},{8,14},{9,15},{10,... | collective-permute-start | bytes 565256 | tf_op jit(solution)/shard_map/ppermute | solution.py:438
  15.3 8.7 %collective-permute-start.6 = (f32[16,2944]{1,0:T(8,128)S(1)}, f32[16,2944]{1,0:T(8,128)S(1)}, u32[]{:S(2)}, u32[]{:S(2)}) collective-permute-start(f32[16,2944]{1,0:T(8,128)S(1)} %get-tuple-element.30.refs_0_), channel_id=1, source_target_pairs={{0,2},{1,3},{2,4},{3,5},{4,6},{5,7},{6,0},{7,1},{8,10},{9,11},{10,... | collective-permute-start | bytes 565256 | tf_op jit(solution)/shard_map/ppermute | solution.py:438
  18.7 5.4 %collective-permute-start.1 = (f32[8,2944]{1,0:T(8,128)S(1)}, f32[8,2944]{1,0:T(8,128)S(1)}, u32[]{:S(2)}, u32[]{:S(2)}) collective-permute-start(f32[8,2944]{1,0:T(8,128)S(1)} %slice.36), channel_id=1, source_target_pairs={{0,6},{1,7},{2,0},{3,1},{4,2},{5,3},{6,4},{7,5},{8,14},{9,15},{10,... | collective-permute-start | bytes 282632 | tf_op jit(solution)/shard_map/ppermute | solution.py:438
  22.2 8.8 %collective-permute-start.8 = (f32[16,2944]{1,0:T(8,128)S(1)}, f32[16,2944]{1,0:T(8,128)S(1)}, u32[]{:S(2)}, u32[]{:S(2)}) collective-permute-start(f32[16,2944]{1,0:T(8,128)S(1)} %get-tuple-element.30.refs_0_), channel_id=1, source_target_pairs={{0,1},{1,0},{2,3},{3,2},{4,5},{5,4},{6,7},{7,6},{8,9},{9,8},{10,11... | collective-permute-start | bytes 565256 | tf_op jit(solution)/shard_map/ppermute | solution.py:438
  24.0 5.6 %collective-permute-start.7 = (f32[8,2944]{1,0:T(8,128)S(1)}, f32[8,2944]{1,0:T(8,128)S(1)}, u32[]{:S(2)}, u32[]{:S(2)}) collective-permute-start(f32[8,2944]{1,0:T(8,128)S(1)} %slice.37), channel_id=1, source_target_pairs={{0,2},{1,3},{2,4},{3,5},{4,6},{5,7},{6,0},{7,1},{8,10},{9,11},{10,... | collective-permute-start | bytes 282632 | tf_op jit(solution)/shard_map/ppermute | solution.py:438
  24.1 6.8 %collective-permute-start.2 = (f32[8,2944]{1,0:T(8,128)S(1)}, f32[8,2944]{1,0:T(8,128)S(1)}, u32[]{:S(2)}, u32[]{:S(2)}) collective-permute-start(f32[8,2944]{1,0:T(8,128)S(1)} %collective-permute-done.1.refs_4_), channel_id=1, source_target_pairs={{0,1},{1,0},{2,3},{3,2},{4,5},{5,4},{6,7},{7,6},{8,9},{9,8},{10,11... | collective-permute-start | bytes 282632 | tf_op jit(solution)/shard_map/ppermute | solution.py:438
  29.7 4.0 %collective-permute-start.11 = (f32[8,2944]{1,0:T(8,128)S(1)}, f32[8,2944]{1,0:T(8,128)S(1)}, u32[]{:S(2)}, u32[]{:S(2)}) collective-permute-start(f32[8,2944]{1,0:T(8,128)S(1)} %collective-permute-done.7.refs_3_), channel_id=1, source_target_pairs={{0,1},{1,0},{2,3},{3,2},{4,5},{5,4},{6,7},{7,6},{8,9},{9,8},{10,11... | collective-permute-start | bytes 282632 | tf_op jit(solution)/shard_map/ppermute | solution.py:438
  30.4 3.3 %collective-permute-start.10 = (f32[16,2944]{1,0:T(8,128)S(1)}, f32[16,2944]{1,0:T(8,128)S(1)}, u32[]{:S(2)}, u32[]{:S(2)}) collective-permute-start(f32[16,2944]{1,0:T(8,128)S(1)} %collective-permute-done.refs_2_), channel_id=1, source_target_pairs={{0,1},{1,0},{2,3},{3,2},{4,5},{5,4},{6,7},{7,6},{8,9},{9,8},{10,11... | collective-permute-start | bytes 565256 | tf_op jit(solution)/shard_map/ppermute | solution.py:438
  30.5 3.3 %collective-permute-start.9 = (f32[16,2944]{1,0:T(8,128)S(1)}, f32[16,2944]{1,0:T(8,128)S(1)}, u32[]{:S(2)}, u32[]{:S(2)}) collective-permute-start(f32[16,2944]{1,0:T(8,128)S(1)} %collective-permute-done.6.refs_1_), channel_id=1, source_target_pairs={{0,1},{1,0},{2,3},{3,2},{4,5},{5,4},{6,7},{7,6},{8,9},{9,8},{10,11... | collective-permute-start | bytes 565256 | tf_op jit(solution)/shard_map/ppermute | solution.py:438
  31.0 20.0 %collective-permute-start.3 = (f32[16,4096]{1,0:T(8,128)S(1)}, f32[16,4096]{1,0:T(8,128)S(1)}, u32[]{:S(2)}, u32[]{:S(2)}) collective-permute-start(f32[16,4096]{1,0:T(8,128)S(1)} %get-tuple-element.38.refs_0_), channel_id=1, source_target_pairs={{0,2},{1,3},{2,4},{3,5},{4,6},{5,7},{6,0},{7,1},{8,10},{9,11},{10,... | collective-permute-start | bytes 786440 | tf_op jit(solution)/shard_map/ppermute | solution.py:438
  31.0 20.0 %collective-permute-start.4 = (f32[16,4096]{1,0:T(8,128)S(1)}, f32[16,4096]{1,0:T(8,128)S(1)}, u32[]{:S(2)}, u32[]{:S(2)}) collective-permute-start(f32[16,4096]{1,0:T(8,128)S(1)} %get-tuple-element.38.refs_0_), channel_id=1, source_target_pairs={{0,6},{1,7},{2,0},{3,1},{4,2},{5,3},{6,4},{7,5},{8,14},{9,15},{10,... | collective-permute-start | bytes 786440 | tf_op jit(solution)/shard_map/ppermute | solution.py:438
  33.6 20.9 %collective-permute-start.5 = (f32[16,4096]{1,0:T(8,128)S(1)}, f32[16,4096]{1,0:T(8,128)S(1)}, u32[]{:S(2)}, u32[]{:S(2)}) collective-permute-start(f32[16,4096]{1,0:T(8,128)S(1)} %get-tuple-element.38.refs_0_), channel_id=1, source_target_pairs={{0,4},{1,5},{2,6},{3,7},{4,0},{5,1},{6,2},{7,3},{8,12},{9,13},{10,... | collective-permute-start | bytes 786440 | tf_op jit(solution)/shard_map/ppermute | solution.py:438
  36.8 2.9 %collective-permute-start.12 = (f32[8,128]{1,0:T(8,128)S(1)}, f32[8,128]{1,0:T(8,128)S(1)}, u32[]{:S(2)}, u32[]{:S(2)}) collective-permute-start(f32[8,128]{1,0:T(8,128)S(1)} %get-tuple-element.33), channel_id=1, source_target_pairs={{0,8},{8,0},{16,24},{24,16},{1,9},{9,1},{17,25},{25,17},{2,10},{10... | collective-permute-start | bytes 12296 | tf_op jit(solution)/shard_map/ppermute | solution.py:438
  41.7 3.0 %collective-permute-start.13 = (f32[16,128]{1,0:T(8,128)S(1)}, f32[16,128]{1,0:T(8,128)S(1)}, u32[]{:S(2)}, u32[]{:S(2)}) collective-permute-start(f32[16,128]{1,0:T(8,128)S(1)} %get-tuple-element.35), channel_id=1, source_target_pairs={{0,8},{8,0},{16,24},{24,16},{1,9},{9,1},{17,25},{25,17},{2,10},{10... | collective-permute-start | bytes 24584 | tf_op jit(solution)/shard_map/ppermute | solution.py:438
  44.7 4.1 %collective-permute-start.14 = (f32[16,128]{1,0:T(8,128)S(1)}, f32[16,128]{1,0:T(8,128)S(1)}, u32[]{:S(2)}, u32[]{:S(2)}) collective-permute-start(f32[16,128]{1,0:T(8,128)S(1)} %add.87), channel_id=1, source_target_pairs={{0,24},{8,16},{16,8},{24,0},{1,25},{9,17},{17,9},{25,1},{2,26},{10... | collective-permute-start | bytes 24584 | tf_op jit(solution)/shard_map/ppermute | solution.py:438
  54.5 10.8 %collective-permute-start.15 = (f32[16,4096]{1,0:T(8,128)S(1)}, f32[16,4096]{1,0:T(8,128)S(1)}, u32[]{:S(2)}, u32[]{:S(2)}) collective-permute-start(f32[16,4096]{1,0:T(8,128)S(1)} %get-tuple-element.38.refs_0_), channel_id=1, source_target_pairs={{0,1},{1,0},{2,3},{3,2},{4,5},{5,4},{6,7},{7,6},{8,9},{9,8},{10,11... | collective-permute-start | bytes 786440 | tf_op jit(solution)/shard_map/ppermute | solution.py:438
  55.7 9.6 %collective-permute-start.16 = (f32[16,4096]{1,0:T(8,128)S(1)}, f32[16,4096]{1,0:T(8,128)S(1)}, u32[]{:S(2)}, u32[]{:S(2)}) collective-permute-start(f32[16,4096]{1,0:T(8,128)S(1)} %collective-permute-done.3.refs_1_), channel_id=1, source_target_pairs={{0,1},{1,0},{2,3},{3,2},{4,5},{5,4},{6,7},{7,6},{8,9},{9,8},{10,11... | collective-permute-start | bytes 786440 | tf_op jit(solution)/shard_map/ppermute | solution.py:438
  55.7 9.6 %collective-permute-start.17 = (f32[16,4096]{1,0:T(8,128)S(1)}, f32[16,4096]{1,0:T(8,128)S(1)}, u32[]{:S(2)}, u32[]{:S(2)}) collective-permute-start(f32[16,4096]{1,0:T(8,128)S(1)} %collective-permute-done.4.refs_2_), channel_id=1, source_target_pairs={{0,1},{1,0},{2,3},{3,2},{4,5},{5,4},{6,7},{7,6},{8,9},{9,8},{10,11... | collective-permute-start | bytes 786440 | tf_op jit(solution)/shard_map/ppermute | solution.py:438
  56.2 9.1 %collective-permute-start.18 = (f32[16,4096]{1,0:T(8,128)S(1)}, f32[16,4096]{1,0:T(8,128)S(1)}, u32[]{:S(2)}, u32[]{:S(2)}) collective-permute-start(f32[16,4096]{1,0:T(8,128)S(1)} %collective-permute-done.5.refs_3_), channel_id=1, source_target_pairs={{0,1},{1,0},{2,3},{3,2},{4,5},{5,4},{6,7},{7,6},{8,9},{9,8},{10,11... | collective-permute-start | bytes 786440 | tf_op jit(solution)/shard_map/ppermute | solution.py:438
  56.2 2.6 %collective-permute-start.19 = (f32[32,128]{1,0:T(8,128)S(1)}, f32[32,128]{1,0:T(8,128)S(1)}, u32[]{:S(2)}, u32[]{:S(2)}) collective-permute-start(f32[32,128]{1,0:T(8,128)S(1)} %get-tuple-element.37), channel_id=1, source_target_pairs={{0,8},{8,0},{16,24},{24,16},{1,9},{9,1},{17,25},{25,17},{2,10},{10... | collective-permute-start | bytes 49160 | tf_op jit(solution)/shard_map/ppermute | solution.py:438
  58.8 3.8 %collective-permute-start.20 = (f32[32,128]{1,0:T(8,128)S(1)}, f32[32,128]{1,0:T(8,128)S(1)}, u32[]{:S(2)}, u32[]{:S(2)}) collective-permute-start(f32[32,128]{1,0:T(8,128)S(1)} %add.89), channel_id=1, source_target_pairs={{0,24},{8,16},{16,8},{24,0},{1,25},{9,17},{17,9},{25,1},{2,26},{10... | collective-permute-start | bytes 49160 | tf_op jit(solution)/shard_map/ppermute | solution.py:438
  62.6 2.7 %collective-permute-start.21 = (f32[32,128]{1,0:T(8,128)S(1)}, f32[32,128]{1,0:T(8,128)S(1)}, u32[]{:S(2)}, u32[]{:S(2)}) collective-permute-start(f32[32,128]{1,0:T(8,128)S(1)} %add.90), channel_id=1, source_target_pairs={{0,32},{32,0},{64,96},{96,64},{128,160},{160,128},{192,224},{224,1... | collective-permute-start | bytes 49160 | tf_op jit(solution)/shard_map/ppermute | solution.py:438
  67.6 3.9 %collective-permute-start.22 = (f32[64,128]{1,0:T(8,128)S(1)}, f32[64,128]{1,0:T(8,128)S(1)}, u32[]{:S(2)}, u32[]{:S(2)}) collective-permute-start(f32[64,128]{1,0:T(8,128)S(1)} %get-tuple-element.44), channel_id=1, source_target_pairs={{0,8},{8,0},{16,24},{24,16},{1,9},{9,1},{17,25},{25,17},{2,10},{10... | collective-permute-start | bytes 98312 | tf_op jit(solution)/shard_map/ppermute | solution.py:438
  71.5 5.1 %collective-permute-start.23 = (f32[64,128]{1,0:T(8,128)S(1)}, f32[64,128]{1,0:T(8,128)S(1)}, u32[]{:S(2)}, u32[]{:S(2)}) collective-permute-start(f32[64,128]{1,0:T(8,128)S(1)} %add.92), channel_id=1, source_target_pairs={{0,24},{8,16},{16,8},{24,0},{1,25},{9,17},{17,9},{25,1},{2,26},{10... | collective-permute-start | bytes 98312 | tf_op jit(solution)/shard_map/ppermute | solution.py:438
  76.5 3.2 %collective-permute-start.24 = (f32[64,128]{1,0:T(8,128)S(1)}, f32[64,128]{1,0:T(8,128)S(1)}, u32[]{:S(2)}, u32[]{:S(2)}) collective-permute-start(f32[64,128]{1,0:T(8,128)S(1)} %add.93), channel_id=1, source_target_pairs={{0,32},{32,0},{64,96},{96,64},{128,160},{160,128},{192,224},{224,1... | collective-permute-start | bytes 98312 | tf_op jit(solution)/shard_map/ppermute | solution.py:438
  79.8 4.2 %collective-permute-start.25 = (f32[64,128]{1,0:T(8,128)S(1)}, f32[64,128]{1,0:T(8,128)S(1)}, u32[]{:S(2)}, u32[]{:S(2)}) collective-permute-start(f32[64,128]{1,0:T(8,128)S(1)} %add.94), channel_id=1, source_target_pairs={{0,64},{32,96},{64,0},{96,32},{128,192},{160,224},{192,128},{224,1... | collective-permute-start | bytes 98312 | tf_op jit(solution)/shard_map/ppermute | solution.py:438
  86.8 5.4 %collective-permute-start.26 = (f32[2,40,128]{2,1,0:T(8,128)S(1)}, f32[2,40,128]{2,1,0:T(8,128)S(1)}, u32[]{:S(2)}, u32[]{:S(2)}) collective-permute-start(f32[2,40,128]{2,1,0:T(8,128)S(1)} %get-tuple-element.47), channel_id=1, source_target_pairs={{0,24},{8,16},{16,8},{24,0},{1,25},{9,17},{17,9},{25,1},{2,26},{10... | collective-permute-start | bytes 122888 | tf_op jit(solution)/shard_map/ppermute | solution.py:438
  92.2 3.5 %collective-permute-start.27 = (f32[40,128]{1,0:T(8,128)S(1)}, f32[40,128]{1,0:T(8,128)S(1)}, u32[]{:S(2)}, u32[]{:S(2)}) collective-permute-start(f32[40,128]{1,0:T(8,128)S(1)} %slice_bitcast_fusion), channel_id=1, source_target_pairs={{0,8},{8,0},{16,24},{24,16},{1,9},{9,1},{17,25},{25,17},{2,10},{10... | collective-permute-start | bytes 61448 | tf_op jit(solution)/shard_map/ppermute | solution.py:438
  95.8 3.1 %collective-permute-start.28 = (f32[32,128]{1,0:T(8,128)S(1)}, f32[32,128]{1,0:T(8,128)S(1)}, u32[]{:S(2)}, u32[]{:S(2)}) collective-permute-start(f32[32,128]{1,0:T(8,128)S(1)} %slice.41), channel_id=1, source_target_pairs={{0,32},{32,0},{64,96},{96,64},{128,160},{160,128},{192,224},{224,1... | collective-permute-start | bytes 49160 | tf_op jit(solution)/shard_map/ppermute | solution.py:438
  98.8 5.2 %collective-permute-start.29 = (f32[32,128]{1,0:T(8,128)S(1)}, f32[32,128]{1,0:T(8,128)S(1)}, u32[]{:S(2)}, u32[]{:S(2)}) collective-permute-start(f32[32,128]{1,0:T(8,128)S(1)} %slice_add_fusion), channel_id=1, source_target_pairs={{0,224},{32,64},{64,32},{96,128},{128,96},{160,192},{192,160},{224... | collective-permute-start | bytes 49160 | tf_op jit(solution)/shard_map/ppermute | solution.py:438
  104.1 4.6 %collective-permute-start.30 = (f32[32,128]{1,0:T(8,128)S(1)}, f32[32,128]{1,0:T(8,128)S(1)}, u32[]{:S(2)}, u32[]{:S(2)}) collective-permute-start(f32[32,128]{1,0:T(8,128)S(1)} %add.99), channel_id=1, source_target_pairs={{0,96},{32,192},{64,160},{96,0},{128,224},{160,64},{192,32},{224,1... | collective-permute-start | bytes 49160 | tf_op jit(solution)/shard_map/ppermute | solution.py:438
  121.9 2.9 %collective-permute-start.31 = (f32[32,128]{1,0:T(8,128)S(1)}, f32[32,128]{1,0:T(8,128)S(1)}, u32[]{:S(2)}, u32[]{:S(2)}) collective-permute-start(f32[32,128]{1,0:T(8,128)S(1)} %shard_map.52), channel_id=1, source_target_pairs={{0,32},{32,0},{64,96},{96,64},{128,160},{160,128},{192,224},{224,1... | collective-permute-start | bytes 49160 | tf_op jit(solution)/shard_map/ppermute | solution.py:438
  124.8 4.2 %collective-permute-start.32 = (f32[32,128]{1,0:T(8,128)S(1)}, f32[32,128]{1,0:T(8,128)S(1)}, u32[]{:S(2)}, u32[]{:S(2)}) collective-permute-start(f32[32,128]{1,0:T(8,128)S(1)} %add.101), channel_id=1, source_target_pairs={{0,224},{32,64},{64,32},{96,128},{128,96},{160,192},{192,160},{224... | collective-permute-start | bytes 49160 | tf_op jit(solution)/shard_map/ppermute | solution.py:438
  129.0 4.4 %collective-permute-start.33 = (f32[32,128]{1,0:T(8,128)S(1)}, f32[32,128]{1,0:T(8,128)S(1)}, u32[]{:S(2)}, u32[]{:S(2)}) collective-permute-start(f32[32,128]{1,0:T(8,128)S(1)} %add.102), channel_id=1, source_target_pairs={{0,96},{32,192},{64,160},{96,0},{128,224},{160,64},{192,32},{224,1... | collective-permute-start | bytes 49160 | tf_op jit(solution)/shard_map/ppermute | solution.py:438
  136.8 2.6 %collective-permute-start.34 = (f32[16,128]{1,0:T(8,128)S(1)}, f32[16,128]{1,0:T(8,128)S(1)}, u32[]{:S(2)}, u32[]{:S(2)}) collective-permute-start(f32[16,128]{1,0:T(8,128)S(1)} %shard_map.53), channel_id=1, source_target_pairs={{0,32},{32,0},{64,96},{96,64},{128,160},{160,128},{192,224},{224,1... | collective-permute-start | bytes 24584 | tf_op jit(solution)/shard_map/ppermute | solution.py:438
  139.4 3.4 %collective-permute-start.35 = (f32[16,128]{1,0:T(8,128)S(1)}, f32[16,128]{1,0:T(8,128)S(1)}, u32[]{:S(2)}, u32[]{:S(2)}) collective-permute-start(f32[16,128]{1,0:T(8,128)S(1)} %add.104), channel_id=1, source_target_pairs={{0,64},{32,96},{64,0},{96,32},{128,192},{160,224},{192,128},{224,1... | collective-permute-start | bytes 24584 | tf_op jit(solution)/shard_map/ppermute | solution.py:438
  145.9 2.8 %collective-permute-start.36 = (f32[8,128]{1,0:T(8,128)S(1)}, f32[8,128]{1,0:T(8,128)S(1)}, u32[]{:S(2)}, u32[]{:S(2)}) collective-permute-start(f32[8,128]{1,0:T(8,128)S(1)} %shard_map.54), channel_id=1, source_target_pairs={{0,32},{32,0},{64,96},{96,64},{128,160},{160,128},{192,224},{224,1... | collective-permute-start | bytes 12296 | tf_op jit(solution)/shard_map/ppermute | solution.py:438
Sparse Core Ops, SparseCore 0:
  11.8 106.3 all-gather.1
where the time goes:
time: 186 us
  waiting for transfers between devices  58.7 us (32%)
  starting transfers between devices  55.3 us (30%)
  Pallas kernels  31 us (17%)
  blocking collectives  21.9 us (12%)
  between operations  13.7 us (7%)
  local copies, waits for them, and re-layouts  4.83 us (3%)
    ppermute x37, starting transfers between devices, moved(): return lax.ppermute(value, axis, [(i, to(i)) for i in range(size)])  55.3 us
    ppermute x37, waiting for transfers between devices, moved(): return lax.ppermute(value, axis, [(i, to(i)) for i in range(size)])  49.1 us
    pallas_call x9, Pallas kernels, call(): pl.pallas_call(body, out_shape=outs, in_specs=specs, out_specs=jax.tree.m...  29.4 us
    all_to_all x1, blocking collectives, local(): out = lax.all_to_all(jnp.transpose(out, (1, 0, 2)), PLANE, 0, 0)  21.9 us
    all_gather x1, waiting for transfers between devices, local(): pack = lax.all_gather(pack, PLANE, axis=0, tiled=True)  9.55 us
  transfers between devices with their start and end apart: 38, of which 25 were waited for; matrix products, arithmetic and copies ran while one was open for 0% of the time, Pallas kernels for 7%

commit v1 on v0

--- a/solution.py
+++ b/solution.py
@@ -21,7 +21,7 @@
 COUNT = (4, 4, 4, 8, 16, 32)
 SPACE = 72
 PATH = 64
-PARTS = (10, 10, 10, 8, 8)
+PARTS = (8, 8, 8, 8, 8)
 RHS_AT = 0
 NAMED_AT = 256
 DIAG_AT = (512, 1152, 1920, 2944, 4480)
@@ -129,7 +129,7 @@
     return pl.ds(pl.multiple_of(d * BLOCK, BLOCK), BLOCK)
 
 
-def couple(off, at, chain, place, first, wide):
+def couple(off, at, chain, place, first, wide, unroll):
     height = SPACE - first
     table = jnp.concatenate(split(chain[first:SPACE, :]), axis=0)
     names, lanes = rows_iota(height, first), small(rows_iota(LANES, 0))
@@ -143,7 +143,7 @@
         wide[block_rows(d), :] = jnp.broadcast_to(-drop, (BLOCK, LANES))
         return carry
 
-    lax.fori_loop(0, BLOCKS, step, 0, unroll=16)
+    lax.fori_loop(0, BLOCKS, step, 0, unroll=unroll)
 
 
 def fetch(pack, held, sems, cuts):
@@ -365,7 +365,7 @@
         copy.wait()
     find_places(named, level, places)
     copies[0].wait()
-    couple(held, columns, chain, places, FIRST[level + 1], wide)
+    couple(held, columns, chain, places, FIRST[level + 1], wide, BLOCKS)
     copies[1].wait()
 
     def write(at, value):
@@ -395,7 +395,7 @@
     for k, level in enumerate((2, 1, 0)):
         find_places(named, level, places)
         copies[2 * k].wait()
-        couple(held, 896 + REACH * level, chain, places, 8, wide)
+        couple(held, 896 + REACH * level, chain, places, 8, wide, BLOCKS // 2)
 
         def write(at, value):
             wide[pl.ds(at, 64), :] = wide[pl.ds(at, 64), :] + value
@@ -476,15 +476,11 @@
     def other_core(parts):
         return parts + tuple(moved(part, "blk", lambda i: i ^ 1) for part in parts)
 
-    half = BLOCK // 2
-    down, up = (moved(first, "blk", lambda i, hop=hop: (i + hop) % SLOTS) for hop in (2, 6))
-    across = (
-        moved(down[:half], "blk", lambda i: (i + 2) % SLOTS),
-        moved(up[half:], "blk", lambda i: (i + 6) % SLOTS),
-    )
-    first = other_core((first, down, up, *across))
-    second = lax.optimization_barrier((second, first[-1]))[0]
-    second = (second,) + tuple(moved(second, "blk", lambda i, hop=hop: (i + hop) % SLOTS) for hop in (2, 6, 4))
+    def this_core(own):
+        return (own,) + tuple(moved(own, "blk", lambda i, hop=hop: (i + hop) % SLOTS) for hop in (2, 6, 4))
+
+    first = other_core(this_core(first))
+    second = this_core(lax.optimization_barrier((second, first[-1]))[0])
 
     def path_scratch(level, *more):
         return [

time: 186 us -> 183 us (0.984)
  waiting for transfers between devices: 58.7 us -> 52.8 us
  starting transfers between devices: 55.3 us -> 59.8 us
    ppermute x37 -> x35, waiting for transfers between devices: 49.1 us -> 43.8 us  [moved(): return lax.ppermute(value, axis, [(i, to(i)) for i in range(size)])]
    ppermute x37 -> x35, starting transfers between devices: 55.3 us -> 59.8 us  [moved(): return lax.ppermute(value, axis, [(i, to(i)) for i in range(size)])]
  transfers between devices with their start and end apart: 38 -> 36, of which waited for: 25 -> 25; matrix products, arithmetic and copies ran while one was open for 0% -> 0% of each run, Pallas kernels for 7% -> 7%
where the time goes in v1:
time: 183 us; the launch traced here: 182 us
  starting transfers between devices  59.8 us (33%)
  waiting for transfers between devices  52.8 us (29%)
  Pallas kernels  30.4 us (17%)
  blocking collectives  20.8 us (11%)
  between operations  13.6 us (7%)
  local copies, waits for them, and re-layouts  4.82 us (3%)
    ppermute x35, starting transfers between devices, moved(): return lax.ppermute(value, axis, [(i, to(i)) for i in range(size)])  59.8 us
    ppermute x35, waiting for transfers between devices, moved(): return lax.ppermute(value, axis, [(i, to(i)) for i in range(size)])  43.8 us
    pallas_call x9, Pallas kernels, call(): pl.pallas_call(body, out_shape=outs, in_specs=specs, out_specs=jax.tree.m...  28.8 us
    all_to_all x1, blocking collectives, local(): out = lax.all_to_all(jnp.transpose(out, (1, 0, 2)), PLANE, 0, 0)  20.8 us
    all_gather x1, waiting for transfers between devices, local(): pack = lax.all_gather(pack, PLANE, axis=0, tiled=True)  9.06 us
  transfers between devices with their start and end apart: 36, of which 25 were waited for; matrix products, arithmetic and copies ran while one was open for 0% of the time, Pallas kernels for 7%

profile of v1, /device:TPU:1, one launch (start us, length us, event | category | flops | bytes accessed | tf_op | source)
XLA Modules:
  0.0 182.4 jit_solution(13084794781055731725)
XLA Ops:
  10.0 1.6 shard_map.46
  11.7 3.8 %collective-permute-start = (f32[16,2944]{1,0:T(8,128)S(1)}, f32[16,2944]{1,0:T(8,128)S(1)}, u32[]{:S(2)}, u32[]{:S(2)}) collective-permute-start(f32[16,2944]{1,0:T(8,128)S(1)} %get-tuple-element.30.refs_0_), channel_id=1, source_target_pairs={{0,4},{1,5},{2,6},{3,7},{4,0},{5,1},{6,2},{7,3},{8,12},{9,13},{10,... | collective-permute-start | bytes 565256 | tf_op jit(solution)/shard_map/ppermute | solution.py:438
  15.9 2.3 %collective-permute-start.6 = (f32[16,2944]{1,0:T(8,128)S(1)}, f32[16,2944]{1,0:T(8,128)S(1)}, u32[]{:S(2)}, u32[]{:S(2)}) collective-permute-start(f32[16,2944]{1,0:T(8,128)S(1)} %get-tuple-element.30.refs_0_), channel_id=1, source_target_pairs={{0,6},{1,7},{2,0},{3,1},{4,2},{5,3},{6,4},{7,5},{8,14},{9,15},{10,... | collective-permute-start | bytes 565256 | tf_op jit(solution)/shard_map/ppermute | solution.py:438
  19.0 4.3 %collective-permute-start.1 = (f32[16,2944]{1,0:T(8,128)S(1)}, f32[16,2944]{1,0:T(8,128)S(1)}, u32[]{:S(2)}, u32[]{:S(2)}) collective-permute-start(f32[16,2944]{1,0:T(8,128)S(1)} %collective-permute-done.refs_3_), channel_id=1, source_target_pairs={{0,1},{1,0},{2,3},{3,2},{4,5},{5,4},{6,7},{7,6},{8,9},{9,8},{10,11... | collective-permute-start | bytes 565256 | tf_op jit(solution)/shard_map/ppermute | solution.py:438
  26.8 1.8 collective-permute-start.3
  29.3 2.9 %shard_map.47 = (f32[256,128]{1,0:T(8,128)S(1)}, f32[8,128]{1,0:T(8,128)S(1)}, f32[4,128]{1,0:T(4,128)S(1)}, s32[5,8,512]{2,1,0:T(8,128)S(1)}) custom-call(f32[16,2944]{1,0:T(8,128)S(1)} %get-tuple-element.30.refs_0_, f32[16,2944]{1,0:T(8,128)S(1)} %collective-permute-done.5.refs_1_, f32[16,2944]{1,0:T(8,128)S(1)} %collective-permute-done.6.refs_2_, ...), custom_call_target="tpu_custom_call" | custom-call | flops 536870912 | bytes 1048576 | tf_op jit(solution)/shard_map/pallas_call | solution.py:421
  33.5 1.7 collective-permute-done.10
  35.2 1.9 %shard_map.48 = (f32[256,128]{1,0:T(8,128)S(1)}, f32[16,128]{1,0:T(8,128)S(1)}) custom-call(f32[16,2944]{1,0:T(8,128)S(1)} %get-tuple-element.30.refs_0_, f32[16,2944]{1,0:T(8,128)S(1)} %collective-permute-done.5.refs_1_, f32[16,2944]{1,0:T(8,128)S(1)} %collective-permute-done.6.refs_2_, f32[16,2944]{1,0:T(8,128)S(1)} %collective-permute-done.refs_3_, ...), custom_call_target="tpu_custom_call" | custom-call | flops 536870912 | bytes 1048576 | tf_op jit(solution)/shard_map/pallas_call | solution.py:421
  38.4 1.7 collective-permute-done.11
  40.1 2.5 %collective-permute-start.12 = (f32[16,128]{1,0:T(8,128)S(1)}, f32[16,128]{1,0:T(8,128)S(1)}, u32[]{:S(2)}, u32[]{:S(2)}) collective-permute-start(f32[16,128]{1,0:T(8,128)S(1)} %add.87), channel_id=1, source_target_pairs={{0,24},{8,16},{16,8},{24,0},{1,25},{9,17},{17,9},{25,1},{2,26},{10... | collective-permute-start | bytes 24584 | tf_op jit(solution)/shard_map/ppermute | solution.py:438
  42.6 1.6 collective-permute-done.12
  44.2 2.0 %shard_map.49 = (f32[256,128]{1,0:T(8,128)S(1)}, f32[32,128]{1,0:T(8,128)S(1)}) custom-call(f32[16,2944]{1,0:T(8,128)S(1)} %get-tuple-element.30.refs_0_, f32[16,2944]{1,0:T(8,128)S(1)} %collective-permute-done.5.refs_1_, f32[16,2944]{1,0:T(8,128)S(1)} %collective-permute-done.6.refs_2_, f32[16,2944]{1,0:T(8,128)S(1)} %collective-permute-done.refs_3_, ...), custom_call_target="tpu_custom_call" | custom-call | flops 536870912 | bytes 1048576 | tf_op jit(solution)/shard_map/pallas_call | solution.py:421
  46.3 3.0 %collective-permute-done.4.refs_3_ = f32[16,4096]{1,0:T(8,128)S(1)} collective-permute-done((f32[16,4096]{1,0:T(8,128)S(1)}, f32[16,4096]{1,0:T(8,128)S(1)}, u32[]{:S(2)}, u32[]{:S(2)}) %collective-permute-start.4) | collective-permute-done | bytes 262176 | tf_op jit(solution)/shard_map/ppermute | solution.py:438
  49.3 1.6 collective-permute-start.13
  52.6 1.4 collective-permute-done.17
  53.9 2.5 %collective-permute-start.18 = (f32[32,128]{1,0:T(8,128)S(1)}, f32[32,128]{1,0:T(8,128)S(1)}, u32[]{:S(2)}, u32[]{:S(2)}) collective-permute-start(f32[32,128]{1,0:T(8,128)S(1)} %add.89), channel_id=1, source_target_pairs={{0,24},{8,16},{16,8},{24,0},{1,25},{9,17},{17,9},{25,1},{2,26},{10... | collective-permute-start | bytes 49160 | tf_op jit(solution)/shard_map/ppermute | solution.py:438
  57.8 2.0 %collective-permute-start.19 = (f32[32,128]{1,0:T(8,128)S(1)}, f32[32,128]{1,0:T(8,128)S(1)}, u32[]{:S(2)}, u32[]{:S(2)}) collective-permute-start(f32[32,128]{1,0:T(8,128)S(1)} %add.90), channel_id=1, source_target_pairs={{0,32},{32,0},{64,96},{96,64},{128,160},{160,128},{192,224},{224,1... | collective-permute-start | bytes 49160 | tf_op jit(solution)/shard_map/ppermute | solution.py:438
  60.9 2.3 %shard_map.50 = (f32[256,128]{1,0:T(8,128)S(1)}, f32[64,128]{1,0:T(8,128)S(1)}) custom-call(f32[16,4096]{1,0:T(8,128)S(1)} %get-tuple-element.38.refs_0_, f32[16,4096]{1,0:T(8,128)S(1)} %collective-permute-done.2.refs_1_, f32[16,4096]{1,0:T(8,128)S(1)} %collective-permute-done.3.refs_2_, f32[16,4096]{1,0:T(8,128)S(1)} %collective-permute-done.4.refs_3_, ...), custom_call_target="tpu_custom_call" | custom-call | flops 536870912 | bytes 1048576 | tf_op jit(solution)/shard_map/pallas_call | solution.py:421
  63.3 2.7 %collective-permute-done.20 = f32[64,128]{1,0:T(8,128)S(1)} collective-permute-done((f32[64,128]{1,0:T(8,128)S(1)}, f32[64,128]{1,0:T(8,128)S(1)}, u32[]{:S(2)}, u32[]{:S(2)}) %collective-permute-start.20) | collective-permute-done | bytes 32800 | tf_op jit(solution)/shard_map/ppermute | solution.py:438
  66.0 2.5 %collective-permute-start.21 = (f32[64,128]{1,0:T(8,128)S(1)}, f32[64,128]{1,0:T(8,128)S(1)}, u32[]{:S(2)}, u32[]{:S(2)}) collective-permute-start(f32[64,128]{1,0:T(8,128)S(1)} %add.92), channel_id=1, source_target_pairs={{0,24},{8,16},{16,8},{24,0},{1,25},{9,17},{17,9},{25,1},{2,26},{10... | collective-permute-start | bytes 98312 | tf_op jit(solution)/shard_map/ppermute | solution.py:438
  68.6 2.3 %collective-permute-done.21 = f32[64,128]{1,0:T(8,128)S(1)} collective-permute-done((f32[64,128]{1,0:T(8,128)S(1)}, f32[64,128]{1,0:T(8,128)S(1)}, u32[]{:S(2)}, u32[]{:S(2)}) %collective-permute-start.21) | collective-permute-done | bytes 32800 | tf_op jit(solution)/shard_map/ppermute | solution.py:438
  70.9 1.5 collective-permute-start.22
  72.5 1.7 collective-permute-done.22
  74.2 4.8 %collective-permute-start.23 = (f32[64,128]{1,0:T(8,128)S(1)}, f32[64,128]{1,0:T(8,128)S(1)}, u32[]{:S(2)}, u32[]{:S(2)}) collective-permute-start(f32[64,128]{1,0:T(8,128)S(1)} %add.94), channel_id=1, source_target_pairs={{0,64},{32,96},{64,0},{96,32},{128,192},{160,224},{192,128},{224,1... | collective-permute-start | bytes 98312 | tf_op jit(solution)/shard_map/ppermute | solution.py:438
  79.0 1.7 collective-permute-done.23
  80.7 2.9 %shard_map.51 = (f32[2,40,128]{2,1,0:T(8,128)S(1)}, f32[2,40,128]{2,1,0:T(8,128)S(1)}, f32[4,128]{1,0:T(4,128)S(1)}, f32[8,128]{1,0:T(8,128)S(1)}, f32[16,128]{1,0:T(8,128)S(1)}) custom-call(f32[16,4096]{1,0:T(8,128)S(1)} %get-tuple-element.38.refs_0_, f32[16,4096]{1,0:T(8,128)S(1)} %collective-permute-done.2.refs_1_, ...), custom_call_target="tpu_custom_call" | custom-call | flops 536870912 | bytes 1048576 | tf_op jit(solution)/shard_map/pallas_call | solution.py:421
  83.6 2.6 %collective-permute-start.24 = (f32[2,40,128]{2,1,0:T(8,128)S(1)}, f32[2,40,128]{2,1,0:T(8,128)S(1)}, u32[]{:S(2)}, u32[]{:S(2)}) collective-permute-start(f32[2,40,128]{2,1,0:T(8,128)S(1)} %get-tuple-element.47), channel_id=1, source_target_pairs={{0,24},{8,16},{16,8},{24,0},{1,25},{9,17},{17,9},{25,1},{2,26},{10... | collective-permute-start | bytes 122888 | tf_op jit(solution)/shard_map/ppermute | solution.py:438
  86.2 2.8 %collective-permute-done.24 = f32[2,40,128]{2,1,0:T(8,128)S(1)} collective-permute-done((f32[2,40,128]{2,1,0:T(8,128)S(1)}, f32[2,40,128]{2,1,0:T(8,128)S(1)}, u32[]{:S(2)}, u32[]{:S(2)}) %collective-permute-start.24) | collective-permute-done | bytes 40992 | tf_op jit(solution)/shard_map/ppermute | solution.py:438
  89.1 3.4 %collective-permute-done.25 = f32[40,128]{1,0:T(8,128)S(1)} collective-permute-done((f32[40,128]{1,0:T(8,128)S(1)}, f32[40,128]{1,0:T(8,128)S(1)}, u32[]{:S(2)}, u32[]{:S(2)}) %collective-permute-start.25) | collective-permute-done | bytes 20512 | tf_op jit(solution)/shard_map/ppermute | solution.py:438
  92.5 1.5 collective-permute-start.26
  94.1 1.5 collective-permute-done.26
  95.6 6.2 %collective-permute-start.27 = (f32[32,128]{1,0:T(8,128)S(1)}, f32[32,128]{1,0:T(8,128)S(1)}, u32[]{:S(2)}, u32[]{:S(2)}) collective-permute-start(f32[32,128]{1,0:T(8,128)S(1)} %slice_add_fusion), channel_id=1, source_target_pairs={{0,224},{32,64},{64,32},{96,128},{128,96},{160,192},{192,160},{224... | collective-permute-start | bytes 49160 | tf_op jit(solution)/shard_map/ppermute | solution.py:438
  101.8 1.5 collective-permute-done.27
  104.1 3.9 %collective-permute-done.28 = f32[32,128]{1,0:T(8,128)S(1)} collective-permute-done((f32[32,128]{1,0:T(8,128)S(1)}, f32[32,128]{1,0:T(8,128)S(1)}, u32[]{:S(2)}, u32[]{:S(2)}) %collective-permute-start.28) | collective-permute-done | bytes 16416 | tf_op jit(solution)/shard_map/ppermute | solution.py:438
  107.9 9.1 %all-gather.2.cloned.1.call-done.pack = f32[512,10880]{1,0:T(8,128)} async-done(((f32[16,10880]{1,0:T(8,128)}), f32[512,10880]{1,0:T(8,128)}) %all-gather.2.cloned.1.call-update) | async-done | bytes 22282256 | tf_op jit(solution)/shard_map/all_gather | solution.py:474
  117.0 3.7 %shard_map.52 = f32[32,128]{1,0:T(8,128)S(1)} custom-call(f32[512,10880]{1,0:T(8,128)} %all-gather.2.cloned.1.call-done.pack, f32[32,128]{1,0:T(8,128)S(1)} %add.100.summed), custom_call_target="tpu_custom_call" | custom-call | flops 536870912 | bytes 1048576 | tf_op jit(solution)/shard_map/pallas_call | solution.py:421
  120.7 1.4 collective-permute-start.29
  123.4 3.0 %collective-permute-start.30 = (f32[32,128]{1,0:T(8,128)S(1)}, f32[32,128]{1,0:T(8,128)S(1)}, u32[]{:S(2)}, u32[]{:S(2)}) collective-permute-start(f32[32,128]{1,0:T(8,128)S(1)} %add.101), channel_id=1, source_target_pairs={{0,224},{32,64},{64,32},{96,128},{128,96},{160,192},{192,160},{224... | collective-permute-start | bytes 49160 | tf_op jit(solution)/shard_map/ppermute | solution.py:438
  127.5 2.9 %collective-permute-start.31 = (f32[32,128]{1,0:T(8,128)S(1)}, f32[32,128]{1,0:T(8,128)S(1)}, u32[]{:S(2)}, u32[]{:S(2)}) collective-permute-start(f32[32,128]{1,0:T(8,128)S(1)} %add.102), channel_id=1, source_target_pairs={{0,96},{32,192},{64,160},{96,0},{128,224},{160,64},{192,32},{224,1... | collective-permute-start | bytes 49160 | tf_op jit(solution)/shard_map/ppermute | solution.py:438
  130.4 1.5 collective-permute-done.31
  131.9 3.4 %shard_map.53 = f32[16,128]{1,0:T(8,128)S(1)} custom-call(f32[512,10880]{1,0:T(8,128)} %all-gather.2.cloned.1.call-done.pack, f32[16,128]{1,0:T(8,128)S(1)} %get-tuple-element.49.residual, f32[32,128]{1,0:T(8,128)S(1)} %add.103.rest_0_.s5), custom_call_target="tpu_custom_call" | custom-call | flops 536870912 | bytes 1048576 | tf_op jit(solution)/shard_map/pallas_call | solution.py:421
  136.4 1.6 collective-permute-done.32
  138.0 1.9 %collective-permute-start.33 = (f32[16,128]{1,0:T(8,128)S(1)}, f32[16,128]{1,0:T(8,128)S(1)}, u32[]{:S(2)}, u32[]{:S(2)}) collective-permute-start(f32[16,128]{1,0:T(8,128)S(1)} %add.104), channel_id=1, source_target_pairs={{0,64},{32,96},{64,0},{96,32},{128,192},{160,224},{192,128},{224,1... | collective-permute-start | bytes 24584 | tf_op jit(solution)/shard_map/ppermute | solution.py:438
  140.0 1.4 collective-permute-done.33
  141.4 2.9 %shard_map.54 = f32[8,128]{1,0:T(8,128)S(1)} custom-call(f32[512,10880]{1,0:T(8,128)} %all-gather.2.cloned.1.call-done.pack, f32[8,128]{1,0:T(8,128)S(1)} %get-tuple-element.50.residual, f32[32,128]{1,0:T(8,128)S(1)} %add.103.rest_0_.s5, f32[16,128]{1,0:T(8,128)S(1)} %add.105.rest_1_.s4), custom_call_target="tpu_custom_call" | custom-call | flops 536870912 | bytes 1048576 | tf_op jit(solution)/shard_map/pallas_call | solution.py:421
  145.3 1.4 collective-permute-done.34
  146.8 6.8 %shard_map.55 = f32[16,128]{1,0:T(8,128)S(1)} custom-call(f32[512,10880]{1,0:T(8,128)} %all-gather.2.cloned.1.call-done.pack, f32[8,128]{1,0:T(8,128)S(1)} %slice.30.r01, f32[4,128]{1,0:T(4,128)S(1)} %get-tuple-element.48.r2, f32[32,128]{1,0:T(8,128)S(1)} %add.103.rest_0_.s5, f32[16,128]{1,0:T(8,128)S(1)} %add.105.rest_1_.s4, f32[8,128]{1,0:T(8,128)S(1)} %add.106.s3), custom_call_target="tpu_custom_call" | custom-call | flops 536870912 | bytes 1048576 | tf_op jit(solution)/shard_map/pallas_call | solution.py:421
  154.0 20.8 %all_to_all.5 = f32[32,6,16]{2,1,0:T(8,128)S(1)} all-to-all(f32[32,6,16]{2,1,0:T(8,128)S(1)} %copy.8), channel_id=1, replica_groups=mesh['z'=8,'x'=4,'blk'=8] {'x','blk'}, dimensions={0} | all-to-all | bytes 24576 | tf_op jit(solution)/shard_map/all_to_all | solution.py:556
  (88 shorter events, 22.4 us)
Async XLA Ops:
  6.5 110.5 %all-gather.2.cloned.1.call-start = ((), (), s32[]{:S(2)}) async-start(), calls=%async_computation.1 | async-start | bytes 22978560 | tf_op jit(solution)/shard_map/all_gather | solution.py:474
  6.5 1.0 copy-start
  7.6 0.9 copy-start.1
  8.5 0.8 copy-start.2
  9.3 0.7 copy-start.3
  11.7 7.3 %collective-permute-start = (f32[16,2944]{1,0:T(8,128)S(1)}, f32[16,2944]{1,0:T(8,128)S(1)}, u32[]{:S(2)}, u32[]{:S(2)}) collective-permute-start(f32[16,2944]{1,0:T(8,128)S(1)} %get-tuple-element.30.refs_0_), channel_id=1, source_target_pairs={{0,4},{1,5},{2,6},{3,7},{4,0},{5,1},{6,2},{7,3},{8,12},{9,13},{10,... | collective-permute-start | bytes 565256 | tf_op jit(solution)/shard_map/ppermute | solution.py:438
  15.5 9.1 %collective-permute-start.5 = (f32[16,2944]{1,0:T(8,128)S(1)}, f32[16,2944]{1,0:T(8,128)S(1)}, u32[]{:S(2)}, u32[]{:S(2)}) collective-permute-start(f32[16,2944]{1,0:T(8,128)S(1)} %get-tuple-element.30.refs_0_), channel_id=1, source_target_pairs={{0,2},{1,3},{2,4},{3,5},{4,6},{5,7},{6,0},{7,1},{8,10},{9,11},{10,... | collective-permute-start | bytes 565256 | tf_op jit(solution)/shard_map/ppermute | solution.py:438
  15.9 10.0 %collective-permute-start.6 = (f32[16,2944]{1,0:T(8,128)S(1)}, f32[16,2944]{1,0:T(8,128)S(1)}, u32[]{:S(2)}, u32[]{:S(2)}) collective-permute-start(f32[16,2944]{1,0:T(8,128)S(1)} %get-tuple-element.30.refs_0_), channel_id=1, source_target_pairs={{0,6},{1,7},{2,0},{3,1},{4,2},{5,3},{6,4},{7,5},{8,14},{9,15},{10,... | collective-permute-start | bytes 565256 | tf_op jit(solution)/shard_map/ppermute | solution.py:438
  19.0 6.9 %collective-permute-start.1 = (f32[16,2944]{1,0:T(8,128)S(1)}, f32[16,2944]{1,0:T(8,128)S(1)}, u32[]{:S(2)}, u32[]{:S(2)}) collective-permute-start(f32[16,2944]{1,0:T(8,128)S(1)} %collective-permute-done.refs_3_), channel_id=1, source_target_pairs={{0,1},{1,0},{2,3},{3,2},{4,5},{5,4},{6,7},{7,6},{8,9},{9,8},{10,11... | collective-permute-start | bytes 565256 | tf_op jit(solution)/shard_map/ppermute | solution.py:438
  23.3 5.3 %collective-permute-start.7 = (f32[16,2944]{1,0:T(8,128)S(1)}, f32[16,2944]{1,0:T(8,128)S(1)}, u32[]{:S(2)}, u32[]{:S(2)}) collective-permute-start(f32[16,2944]{1,0:T(8,128)S(1)} %get-tuple-element.30.refs_0_), channel_id=1, source_target_pairs={{0,1},{1,0},{2,3},{3,2},{4,5},{5,4},{6,7},{7,6},{8,9},{9,8},{10,11... | collective-permute-start | bytes 565256 | tf_op jit(solution)/shard_map/ppermute | solution.py:438
  24.6 4.7 %collective-permute-start.8 = (f32[16,2944]{1,0:T(8,128)S(1)}, f32[16,2944]{1,0:T(8,128)S(1)}, u32[]{:S(2)}, u32[]{:S(2)}) collective-permute-start(f32[16,2944]{1,0:T(8,128)S(1)} %collective-permute-done.5.refs_1_), channel_id=1, source_target_pairs={{0,1},{1,0},{2,3},{3,2},{4,5},{5,4},{6,7},{7,6},{8,9},{9,8},{10,11... | collective-permute-start | bytes 565256 | tf_op jit(solution)/shard_map/ppermute | solution.py:438
  25.9 3.4 %collective-permute-start.9 = (f32[16,2944]{1,0:T(8,128)S(1)}, f32[16,2944]{1,0:T(8,128)S(1)}, u32[]{:S(2)}, u32[]{:S(2)}) collective-permute-start(f32[16,2944]{1,0:T(8,128)S(1)} %collective-permute-done.6.refs_2_), channel_id=1, source_target_pairs={{0,1},{1,0},{2,3},{3,2},{4,5},{5,4},{6,7},{7,6},{8,9},{9,8},{10,11... | collective-permute-start | bytes 565256 | tf_op jit(solution)/shard_map/ppermute | solution.py:438
  25.9 20.3 %collective-permute-start.2 = (f32[16,4096]{1,0:T(8,128)S(1)}, f32[16,4096]{1,0:T(8,128)S(1)}, u32[]{:S(2)}, u32[]{:S(2)}) collective-permute-start(f32[16,4096]{1,0:T(8,128)S(1)} %get-tuple-element.38.refs_0_), channel_id=1, source_target_pairs={{0,2},{1,3},{2,4},{3,5},{4,6},{5,7},{6,0},{7,1},{8,10},{9,11},{10,... | collective-permute-start | bytes 786440 | tf_op jit(solution)/shard_map/ppermute | solution.py:438
  26.8 19.4 %collective-permute-start.3 = (f32[16,4096]{1,0:T(8,128)S(1)}, f32[16,4096]{1,0:T(8,128)S(1)}, u32[]{:S(2)}, u32[]{:S(2)}) collective-permute-start(f32[16,4096]{1,0:T(8,128)S(1)} %get-tuple-element.38.refs_0_), channel_id=1, source_target_pairs={{0,6},{1,7},{2,0},{3,1},{4,2},{5,3},{6,4},{7,5},{8,14},{9,15},{10,... | collective-permute-start | bytes 786440 | tf_op jit(solution)/shard_map/ppermute | solution.py:438
  28.6 20.6 %collective-permute-start.4 = (f32[16,4096]{1,0:T(8,128)S(1)}, f32[16,4096]{1,0:T(8,128)S(1)}, u32[]{:S(2)}, u32[]{:S(2)}) collective-permute-start(f32[16,4096]{1,0:T(8,128)S(1)} %get-tuple-element.38.refs_0_), channel_id=1, source_target_pairs={{0,4},{1,5},{2,6},{3,7},{4,0},{5,1},{6,2},{7,3},{8,12},{9,13},{10,... | collective-permute-start | bytes 786440 | tf_op jit(solution)/shard_map/ppermute | solution.py:438
  32.2 3.0 %collective-permute-start.10 = (f32[8,128]{1,0:T(8,128)S(1)}, f32[8,128]{1,0:T(8,128)S(1)}, u32[]{:S(2)}, u32[]{:S(2)}) collective-permute-start(f32[8,128]{1,0:T(8,128)S(1)} %get-tuple-element.33), channel_id=1, source_target_pairs={{0,8},{8,0},{16,24},{24,16},{1,9},{9,1},{17,25},{25,17},{2,10},{10... | collective-permute-start | bytes 12296 | tf_op jit(solution)/shard_map/ppermute | solution.py:438
  37.1 3.0 %collective-permute-start.11 = (f32[16,128]{1,0:T(8,128)S(1)}, f32[16,128]{1,0:T(8,128)S(1)}, u32[]{:S(2)}, u32[]{:S(2)}) collective-permute-start(f32[16,128]{1,0:T(8,128)S(1)} %get-tuple-element.35), channel_id=1, source_target_pairs={{0,8},{8,0},{16,24},{24,16},{1,9},{9,1},{17,25},{25,17},{2,10},{10... | collective-permute-start | bytes 24584 | tf_op jit(solution)/shard_map/ppermute | solution.py:438
  40.1 4.1 %collective-permute-start.12 = (f32[16,128]{1,0:T(8,128)S(1)}, f32[16,128]{1,0:T(8,128)S(1)}, u32[]{:S(2)}, u32[]{:S(2)}) collective-permute-start(f32[16,128]{1,0:T(8,128)S(1)} %add.87), channel_id=1, source_target_pairs={{0,24},{8,16},{16,8},{24,0},{1,25},{9,17},{17,9},{25,1},{2,26},{10... | collective-permute-start | bytes 24584 | tf_op jit(solution)/shard_map/ppermute | solution.py:438
  49.3 11.6 %collective-permute-start.13 = (f32[16,4096]{1,0:T(8,128)S(1)}, f32[16,4096]{1,0:T(8,128)S(1)}, u32[]{:S(2)}, u32[]{:S(2)}) collective-permute-start(f32[16,4096]{1,0:T(8,128)S(1)} %get-tuple-element.38.refs_0_), channel_id=1, source_target_pairs={{0,1},{1,0},{2,3},{3,2},{4,5},{5,4},{6,7},{7,6},{8,9},{9,8},{10,11... | collective-permute-start | bytes 786440 | tf_op jit(solution)/shard_map/ppermute | solution.py:438
  50.8 10.1 %collective-permute-start.14 = (f32[16,4096]{1,0:T(8,128)S(1)}, f32[16,4096]{1,0:T(8,128)S(1)}, u32[]{:S(2)}, u32[]{:S(2)}) collective-permute-start(f32[16,4096]{1,0:T(8,128)S(1)} %collective-permute-done.2.refs_1_), channel_id=1, source_target_pairs={{0,1},{1,0},{2,3},{3,2},{4,5},{5,4},{6,7},{7,6},{8,9},{9,8},{10,11... | collective-permute-start | bytes 786440 | tf_op jit(solution)/shard_map/ppermute | solution.py:438
  50.8 10.1 %collective-permute-start.15 = (f32[16,4096]{1,0:T(8,128)S(1)}, f32[16,4096]{1,0:T(8,128)S(1)}, u32[]{:S(2)}, u32[]{:S(2)}) collective-permute-start(f32[16,4096]{1,0:T(8,128)S(1)} %collective-permute-done.3.refs_2_), channel_id=1, source_target_pairs={{0,1},{1,0},{2,3},{3,2},{4,5},{5,4},{6,7},{7,6},{8,9},{9,8},{10,11... | collective-permute-start | bytes 786440 | tf_op jit(solution)/shard_map/ppermute | solution.py:438
  51.3 9.6 %collective-permute-start.16 = (f32[16,4096]{1,0:T(8,128)S(1)}, f32[16,4096]{1,0:T(8,128)S(1)}, u32[]{:S(2)}, u32[]{:S(2)}) collective-permute-start(f32[16,4096]{1,0:T(8,128)S(1)} %collective-permute-done.4.refs_3_), channel_id=1, source_target_pairs={{0,1},{1,0},{2,3},{3,2},{4,5},{5,4},{6,7},{7,6},{8,9},{9,8},{10,11... | collective-permute-start | bytes 786440 | tf_op jit(solution)/shard_map/ppermute | solution.py:438
  51.4 2.6 %collective-permute-start.17 = (f32[32,128]{1,0:T(8,128)S(1)}, f32[32,128]{1,0:T(8,128)S(1)}, u32[]{:S(2)}, u32[]{:S(2)}) collective-permute-start(f32[32,128]{1,0:T(8,128)S(1)} %get-tuple-element.37), channel_id=1, source_target_pairs={{0,8},{8,0},{16,24},{24,16},{1,9},{9,1},{17,25},{25,17},{2,10},{10... | collective-permute-start | bytes 49160 | tf_op jit(solution)/shard_map/ppermute | solution.py:438
  53.9 3.8 %collective-permute-start.18 = (f32[32,128]{1,0:T(8,128)S(1)}, f32[32,128]{1,0:T(8,128)S(1)}, u32[]{:S(2)}, u32[]{:S(2)}) collective-permute-start(f32[32,128]{1,0:T(8,128)S(1)} %add.89), channel_id=1, source_target_pairs={{0,24},{8,16},{16,8},{24,0},{1,25},{9,17},{17,9},{25,1},{2,26},{10... | collective-permute-start | bytes 49160 | tf_op jit(solution)/shard_map/ppermute | solution.py:438
  57.8 3.1 %collective-permute-start.19 = (f32[32,128]{1,0:T(8,128)S(1)}, f32[32,128]{1,0:T(8,128)S(1)}, u32[]{:S(2)}, u32[]{:S(2)}) collective-permute-start(f32[32,128]{1,0:T(8,128)S(1)} %add.90), channel_id=1, source_target_pairs={{0,32},{32,0},{64,96},{96,64},{128,160},{160,128},{192,224},{224,1... | collective-permute-start | bytes 49160 | tf_op jit(solution)/shard_map/ppermute | solution.py:438
  63.2 2.9 %collective-permute-start.20 = (f32[64,128]{1,0:T(8,128)S(1)}, f32[64,128]{1,0:T(8,128)S(1)}, u32[]{:S(2)}, u32[]{:S(2)}) collective-permute-start(f32[64,128]{1,0:T(8,128)S(1)} %get-tuple-element.44), channel_id=1, source_target_pairs={{0,8},{8,0},{16,24},{24,16},{1,9},{9,1},{17,25},{25,17},{2,10},{10... | collective-permute-start | bytes 98312 | tf_op jit(solution)/shard_map/ppermute | solution.py:438
  66.0 4.9 %collective-permute-start.21 = (f32[64,128]{1,0:T(8,128)S(1)}, f32[64,128]{1,0:T(8,128)S(1)}, u32[]{:S(2)}, u32[]{:S(2)}) collective-permute-start(f32[64,128]{1,0:T(8,128)S(1)} %add.92), channel_id=1, source_target_pairs={{0,24},{8,16},{16,8},{24,0},{1,25},{9,17},{17,9},{25,1},{2,26},{10... | collective-permute-start | bytes 98312 | tf_op jit(solution)/shard_map/ppermute | solution.py:438
  70.9 3.2 %collective-permute-start.22 = (f32[64,128]{1,0:T(8,128)S(1)}, f32[64,128]{1,0:T(8,128)S(1)}, u32[]{:S(2)}, u32[]{:S(2)}) collective-permute-start(f32[64,128]{1,0:T(8,128)S(1)} %add.93), channel_id=1, source_target_pairs={{0,32},{32,0},{64,96},{96,64},{128,160},{160,128},{192,224},{224,1... | collective-permute-start | bytes 98312 | tf_op jit(solution)/shard_map/ppermute | solution.py:438
  74.2 6.5 %collective-permute-start.23 = (f32[64,128]{1,0:T(8,128)S(1)}, f32[64,128]{1,0:T(8,128)S(1)}, u32[]{:S(2)}, u32[]{:S(2)}) collective-permute-start(f32[64,128]{1,0:T(8,128)S(1)} %add.94), channel_id=1, source_target_pairs={{0,64},{32,96},{64,0},{96,32},{128,192},{160,224},{192,128},{224,1... | collective-permute-start | bytes 98312 | tf_op jit(solution)/shard_map/ppermute | solution.py:438
  83.6 5.4 %collective-permute-start.24 = (f32[2,40,128]{2,1,0:T(8,128)S(1)}, f32[2,40,128]{2,1,0:T(8,128)S(1)}, u32[]{:S(2)}, u32[]{:S(2)}) collective-permute-start(f32[2,40,128]{2,1,0:T(8,128)S(1)} %get-tuple-element.47), channel_id=1, source_target_pairs={{0,24},{8,16},{16,8},{24,0},{1,25},{9,17},{17,9},{25,1},{2,26},{10... | collective-permute-start | bytes 122888 | tf_op jit(solution)/shard_map/ppermute | solution.py:438
  89.0 3.5 %collective-permute-start.25 = (f32[40,128]{1,0:T(8,128)S(1)}, f32[40,128]{1,0:T(8,128)S(1)}, u32[]{:S(2)}, u32[]{:S(2)}) collective-permute-start(f32[40,128]{1,0:T(8,128)S(1)} %slice_bitcast_fusion), channel_id=1, source_target_pairs={{0,8},{8,0},{16,24},{24,16},{1,9},{9,1},{17,25},{25,17},{2,10},{10... | collective-permute-start | bytes 61448 | tf_op jit(solution)/shard_map/ppermute | solution.py:438
  92.5 3.1 %collective-permute-start.26 = (f32[32,128]{1,0:T(8,128)S(1)}, f32[32,128]{1,0:T(8,128)S(1)}, u32[]{:S(2)}, u32[]{:S(2)}) collective-permute-start(f32[32,128]{1,0:T(8,128)S(1)} %slice.31), channel_id=1, source_target_pairs={{0,32},{32,0},{64,96},{96,64},{128,160},{160,128},{192,224},{224,1... | collective-permute-start | bytes 49160 | tf_op jit(solution)/shard_map/ppermute | solution.py:438
  95.6 7.7 %collective-permute-start.27 = (f32[32,128]{1,0:T(8,128)S(1)}, f32[32,128]{1,0:T(8,128)S(1)}, u32[]{:S(2)}, u32[]{:S(2)}) collective-permute-start(f32[32,128]{1,0:T(8,128)S(1)} %slice_add_fusion), channel_id=1, source_target_pairs={{0,224},{32,64},{64,32},{96,128},{128,96},{160,192},{192,160},{224... | collective-permute-start | bytes 49160 | tf_op jit(solution)/shard_map/ppermute | solution.py:438
  103.3 4.6 %collective-permute-start.28 = (f32[32,128]{1,0:T(8,128)S(1)}, f32[32,128]{1,0:T(8,128)S(1)}, u32[]{:S(2)}, u32[]{:S(2)}) collective-permute-start(f32[32,128]{1,0:T(8,128)S(1)} %add.99), channel_id=1, source_target_pairs={{0,96},{32,192},{64,160},{96,0},{128,224},{160,64},{192,32},{224,1... | collective-permute-start | bytes 49160 | tf_op jit(solution)/shard_map/ppermute | solution.py:438
  120.7 2.7 %collective-permute-start.29 = (f32[32,128]{1,0:T(8,128)S(1)}, f32[32,128]{1,0:T(8,128)S(1)}, u32[]{:S(2)}, u32[]{:S(2)}) collective-permute-start(f32[32,128]{1,0:T(8,128)S(1)} %shard_map.52), channel_id=1, source_target_pairs={{0,32},{32,0},{64,96},{96,64},{128,160},{160,128},{192,224},{224,1... | collective-permute-start | bytes 49160 | tf_op jit(solution)/shard_map/ppermute | solution.py:438
  123.4 4.2 %collective-permute-start.30 = (f32[32,128]{1,0:T(8,128)S(1)}, f32[32,128]{1,0:T(8,128)S(1)}, u32[]{:S(2)}, u32[]{:S(2)}) collective-permute-start(f32[32,128]{1,0:T(8,128)S(1)} %add.101), channel_id=1, source_target_pairs={{0,224},{32,64},{64,32},{96,128},{128,96},{160,192},{192,160},{224... | collective-permute-start | bytes 49160 | tf_op jit(solution)/shard_map/ppermute | solution.py:438
  127.5 4.4 %collective-permute-start.31 = (f32[32,128]{1,0:T(8,128)S(1)}, f32[32,128]{1,0:T(8,128)S(1)}, u32[]{:S(2)}, u32[]{:S(2)}) collective-permute-start(f32[32,128]{1,0:T(8,128)S(1)} %add.102), channel_id=1, source_target_pairs={{0,96},{32,192},{64,160},{96,0},{128,224},{160,64},{192,32},{224,1... | collective-permute-start | bytes 49160 | tf_op jit(solution)/shard_map/ppermute | solution.py:438
  135.4 2.6 %collective-permute-start.32 = (f32[16,128]{1,0:T(8,128)S(1)}, f32[16,128]{1,0:T(8,128)S(1)}, u32[]{:S(2)}, u32[]{:S(2)}) collective-permute-start(f32[16,128]{1,0:T(8,128)S(1)} %shard_map.53), channel_id=1, source_target_pairs={{0,32},{32,0},{64,96},{96,64},{128,160},{160,128},{192,224},{224,1... | collective-permute-start | bytes 24584 | tf_op jit(solution)/shard_map/ppermute | solution.py:438
  138.0 3.4 %collective-permute-start.33 = (f32[16,128]{1,0:T(8,128)S(1)}, f32[16,128]{1,0:T(8,128)S(1)}, u32[]{:S(2)}, u32[]{:S(2)}) collective-permute-start(f32[16,128]{1,0:T(8,128)S(1)} %add.104), channel_id=1, source_target_pairs={{0,64},{32,96},{64,0},{96,32},{128,192},{160,224},{192,128},{224,1... | collective-permute-start | bytes 24584 | tf_op jit(solution)/shard_map/ppermute | solution.py:438
  144.2 2.5 %collective-permute-start.34 = (f32[8,128]{1,0:T(8,128)S(1)}, f32[8,128]{1,0:T(8,128)S(1)}, u32[]{:S(2)}, u32[]{:S(2)}) collective-permute-start(f32[8,128]{1,0:T(8,128)S(1)} %shard_map.54), channel_id=1, source_target_pairs={{0,32},{32,0},{64,96},{96,64},{128,160},{160,128},{192,224},{224,1... | collective-permute-start | bytes 12296 | tf_op jit(solution)/shard_map/ppermute | solution.py:438
Sparse Core Ops, SparseCore 0:
  11.8 105.1 all-gather.1

commit v2 on v1

--- a/solution.py
+++ b/solution.py
@@ -395,7 +395,7 @@
     for k, level in enumerate((2, 1, 0)):
         find_places(named, level, places)
         copies[2 * k].wait()
-        couple(held, 896 + REACH * level, chain, places, 8, wide, BLOCKS // 2)
+        couple(held, 896 + REACH * level, chain, places, 8, wide, BLOCKS)
 
         def write(at, value):
             wide[pl.ds(at, 64), :] = wide[pl.ds(at, 64), :] + value
@@ -469,7 +469,7 @@
         in_specs=[vmem, vmem, hbm, hbm],
         out_specs=(vmem,) * 3,
         scratch_shapes=[pltpu.SemaphoreType.DMA((16,))],
-        compiler_params=pltpu.CompilerParams(vmem_limit_bytes=6 * MIB),
+        compiler_params=pltpu.CompilerParams(vmem_limit_bytes=56 * MIB),
     )(jnp.transpose(rhs, (0, 2, 1)), rows_index, diag_inverse, off_diagonal)
     pack = lax.all_gather(pack, PLANE, axis=0, tiled=True)
 

time: 183 us -> 182 us (level)
  waiting for transfers between devices: 52.8 us -> 50.3 us
    unnamed x13 -> x15, local copies, waits for them, and re-layouts: 3.47 us -> 4.75 us
where the time goes in v2:
time: 182 us
  starting transfers between devices  58.1 us (32%)
  waiting for transfers between devices  50.3 us (28%)
  Pallas kernels  31.3 us (17%)
  blocking collectives  22.4 us (12%)
  between operations  13.7 us (8%)
  local copies, waits for them, and re-layouts  6.09 us (3%)
    ppermute x35, starting transfers between devices, moved(): return lax.ppermute(value, axis, [(i, to(i)) for i in range(size)])  58.1 us
    ppermute x35, waiting for transfers between devices, moved(): return lax.ppermute(value, axis, [(i, to(i)) for i in range(size)])  43 us
    pallas_call x9, Pallas kernels, call(): pl.pallas_call(body, out_shape=outs, in_specs=specs, out_specs=jax.tree.m...  28 us
    all_to_all x1, blocking collectives, local(): out = lax.all_to_all(jnp.transpose(out, (1, 0, 2)), PLANE, 0, 0)  22.4 us
    all_gather x1, waiting for transfers between devices, local(): pack = lax.all_gather(pack, PLANE, axis=0, tiled=True)  7.25 us
    unnamed x15, local copies, waits for them, and re-layouts  4.75 us
  transfers between devices with their start and end apart: 36, of which 25 were waited for; matrix products, arithmetic and copies ran while one was open for 0% of the time, Pallas kernels for 7%

profile of v2, /device:TPU:1, one launch (start us, length us, event | category | flops | bytes accessed | tf_op | source)
XLA Modules:
  0.0 181.9 jit_solution(16349204413570683329)
XLA Ops:
  6.5 3.3 %shard_map.46 = (f32[16,10880]{1,0:T(8,128)}, f32[16,2944]{1,0:T(8,128)}, f32[16,4096]{1,0:T(8,128)}) custom-call(f32[6,16,32]{2,1,0:T(8,128)} %bitcast.18, s32[5,1,512]{2,1,0:T(1,128)} %rows_index.1, f32[16,8064]{1,0:T(8,128)} %diag_inverse.1, f32[5,16,512]{2,1,0:T(8,128)} %off_diagonal.1), custom_call_target="tpu_custom_call" | custom-call | tf_op jit(solution)/shard_map/pallas_call | solution.py:466
  9.8 3.8 %collective-permute-start = (f32[16,2944]{1,0:T(8,128)}, f32[16,2944]{1,0:T(8,128)S(1)}, u32[]{:S(2)}, u32[]{:S(2)}) collective-permute-start(f32[16,2944]{1,0:T(8,128)} %get-tuple-element.30.refs_0_), channel_id=1, source_target_pairs={{0,4},{1,5},{2,6},{3,7},{4,0},{5,1},{6,2},{7,3},{8,12},{9,13},{10,... | collective-permute-start | bytes 565256 | tf_op jit(solution)/shard_map/ppermute | solution.py:438
  14.1 2.3 %collective-permute-start.6 = (f32[16,2944]{1,0:T(8,128)}, f32[16,2944]{1,0:T(8,128)S(1)}, u32[]{:S(2)}, u32[]{:S(2)}) collective-permute-start(f32[16,2944]{1,0:T(8,128)} %get-tuple-element.30.refs_0_), channel_id=1, source_target_pairs={{0,6},{1,7},{2,0},{3,1},{4,2},{5,3},{6,4},{7,5},{8,14},{9,15},{10,... | collective-permute-start | bytes 565256 | tf_op jit(solution)/shard_map/ppermute | solution.py:438
  17.5 4.2 %collective-permute-start.1 = (f32[16,2944]{1,0:T(8,128)S(1)}, f32[16,2944]{1,0:T(8,128)S(1)}, u32[]{:S(2)}, u32[]{:S(2)}) collective-permute-start(f32[16,2944]{1,0:T(8,128)S(1)} %collective-permute-done.refs_3_), channel_id=1, source_target_pairs={{0,1},{1,0},{2,3},{3,2},{4,5},{5,4},{6,7},{7,6},{8,9},{9,8},{10,11... | collective-permute-start | bytes 565256 | tf_op jit(solution)/shard_map/ppermute | solution.py:438
  25.2 1.8 %collective-permute-start.3 = (f32[16,4096]{1,0:T(8,128)}, f32[16,4096]{1,0:T(8,128)S(1)}, u32[]{:S(2)}, u32[]{:S(2)}) collective-permute-start(f32[16,4096]{1,0:T(8,128)} %get-tuple-element.38.refs_0_), channel_id=1, source_target_pairs={{0,6},{1,7},{2,0},{3,1},{4,2},{5,3},{6,4},{7,5},{8,14},{9,15},{10,... | collective-permute-start | bytes 786440 | tf_op jit(solution)/shard_map/ppermute | solution.py:438
  28.6 2.9 %shard_map.47 = (f32[256,128]{1,0:T(8,128)S(1)}, f32[8,128]{1,0:T(8,128)S(1)}, f32[4,128]{1,0:T(4,128)S(1)}, s32[5,8,512]{2,1,0:T(8,128)S(1)}) custom-call(f32[16,2944]{1,0:T(8,128)S(1)} %copy-done.2, f32[16,2944]{1,0:T(8,128)S(1)} %collective-permute-done.5.refs_1_, f32[16,2944]{1,0:T(8,128)S(1)} %collective-permute-done.6.refs_2_, ...), custom_call_target="tpu_custom_call" | custom-call | flops 536870912 | bytes 1048576 | tf_op jit(solution)/shard_map/pallas_call | solution.py:421
  32.9 1.7 collective-permute-done.10
  35.4 1.9 %shard_map.48 = (f32[256,128]{1,0:T(8,128)S(1)}, f32[16,128]{1,0:T(8,128)S(1)}) custom-call(f32[16,2944]{1,0:T(8,128)S(1)} %copy-done.3, f32[16,2944]{1,0:T(8,128)S(1)} %collective-permute-done.5.refs_1_, f32[16,2944]{1,0:T(8,128)S(1)} %collective-permute-done.6.refs_2_, f32[16,2944]{1,0:T(8,128)S(1)} %collective-permute-done.refs_3_, ...), custom_call_target="tpu_custom_call" | custom-call | flops 536870912 | bytes 1048576 | tf_op jit(solution)/shard_map/pallas_call | solution.py:421
  38.7 1.7 collective-permute-done.11
  40.4 2.5 %collective-permute-start.12 = (f32[16,128]{1,0:T(8,128)S(1)}, f32[16,128]{1,0:T(8,128)S(1)}, u32[]{:S(2)}, u32[]{:S(2)}) collective-permute-start(f32[16,128]{1,0:T(8,128)S(1)} %add.87), channel_id=1, source_target_pairs={{0,24},{8,16},{16,8},{24,0},{1,25},{9,17},{17,9},{25,1},{2,26},{10... | collective-permute-start | bytes 24584 | tf_op jit(solution)/shard_map/ppermute | solution.py:438
  42.8 1.6 collective-permute-done.12
  45.4 2.0 %shard_map.49 = (f32[256,128]{1,0:T(8,128)S(1)}, f32[32,128]{1,0:T(8,128)S(1)}) custom-call(f32[16,2944]{1,0:T(8,128)S(1)} %copy-done.4, f32[16,2944]{1,0:T(8,128)S(1)} %collective-permute-done.5.refs_1_, f32[16,2944]{1,0:T(8,128)S(1)} %collective-permute-done.6.refs_2_, f32[16,2944]{1,0:T(8,128)S(1)} %collective-permute-done.refs_3_, ...), custom_call_target="tpu_custom_call" | custom-call | flops 536870912 | bytes 1048576 | tf_op jit(solution)/shard_map/pallas_call | solution.py:421
  48.3 2.5 %collective-permute-start.13 = (f32[16,4096]{1,0:T(8,128)}, f32[16,4096]{1,0:T(8,128)S(1)}, u32[]{:S(2)}, u32[]{:S(2)}) collective-permute-start(f32[16,4096]{1,0:T(8,128)} %get-tuple-element.38.refs_0_), channel_id=1, source_target_pairs={{0,1},{1,0},{2,3},{3,2},{4,5},{5,4},{6,7},{7,6},{8,9},{9,8},{10,11... | collective-permute-start | bytes 786440 | tf_op jit(solution)/shard_map/ppermute | solution.py:438
  51.6 2.4 %collective-permute-done.17 = f32[32,128]{1,0:T(8,128)S(1)} collective-permute-done((f32[32,128]{1,0:T(8,128)S(1)}, f32[32,128]{1,0:T(8,128)S(1)}, u32[]{:S(2)}, u32[]{:S(2)}) %collective-permute-start.17) | collective-permute-done | bytes 16416 | tf_op jit(solution)/shard_map/ppermute | solution.py:438
  54.0 2.5 %collective-permute-start.18 = (f32[32,128]{1,0:T(8,128)S(1)}, f32[32,128]{1,0:T(8,128)S(1)}, u32[]{:S(2)}, u32[]{:S(2)}) collective-permute-start(f32[32,128]{1,0:T(8,128)S(1)} %add.89), channel_id=1, source_target_pairs={{0,24},{8,16},{16,8},{24,0},{1,25},{9,17},{17,9},{25,1},{2,26},{10... | collective-permute-start | bytes 49160 | tf_op jit(solution)/shard_map/ppermute | solution.py:438
  56.4 1.3 collective-permute-done.18
  57.8 1.7 collective-permute-start.19
  61.6 2.2 %shard_map.50 = (f32[256,128]{1,0:T(8,128)S(1)}, f32[64,128]{1,0:T(8,128)S(1)}) custom-call(f32[16,4096]{1,0:T(8,128)S(1)} %copy-done, f32[16,4096]{1,0:T(8,128)S(1)} %collective-permute-done.2.refs_1_, f32[16,4096]{1,0:T(8,128)S(1)} %collective-permute-done.3.refs_2_, f32[16,4096]{1,0:T(8,128)S(1)} %collective-permute-done.4.refs_3_, ...), custom_call_target="tpu_custom_call" | custom-call | flops 536870912 | bytes 1048576 | tf_op jit(solution)/shard_map/pallas_call | solution.py:421
  64.0 3.5 %collective-permute-done.20 = f32[64,128]{1,0:T(8,128)S(1)} collective-permute-done((f32[64,128]{1,0:T(8,128)S(1)}, f32[64,128]{1,0:T(8,128)S(1)}, u32[]{:S(2)}, u32[]{:S(2)}) %collective-permute-start.20) | collective-permute-done | bytes 32800 | tf_op jit(solution)/shard_map/ppermute | solution.py:438
  67.5 2.5 %collective-permute-start.21 = (f32[64,128]{1,0:T(8,128)S(1)}, f32[64,128]{1,0:T(8,128)S(1)}, u32[]{:S(2)}, u32[]{:S(2)}) collective-permute-start(f32[64,128]{1,0:T(8,128)S(1)} %add.92), channel_id=1, source_target_pairs={{0,24},{8,16},{16,8},{24,0},{1,25},{9,17},{17,9},{25,1},{2,26},{10... | collective-permute-start | bytes 98312 | tf_op jit(solution)/shard_map/ppermute | solution.py:438
  70.0 2.5 %collective-permute-done.21 = f32[64,128]{1,0:T(8,128)S(1)} collective-permute-done((f32[64,128]{1,0:T(8,128)S(1)}, f32[64,128]{1,0:T(8,128)S(1)}, u32[]{:S(2)}, u32[]{:S(2)}) %collective-permute-start.21) | collective-permute-done | bytes 32800 | tf_op jit(solution)/shard_map/ppermute | solution.py:438
  72.5 1.5 collective-permute-start.22
  74.1 1.7 collective-permute-done.22
  75.8 3.4 %collective-permute-start.23 = (f32[64,128]{1,0:T(8,128)S(1)}, f32[64,128]{1,0:T(8,128)S(1)}, u32[]{:S(2)}, u32[]{:S(2)}) collective-permute-start(f32[64,128]{1,0:T(8,128)S(1)} %add.94), channel_id=1, source_target_pairs={{0,64},{32,96},{64,0},{96,32},{128,192},{160,224},{192,128},{224,1... | collective-permute-start | bytes 98312 | tf_op jit(solution)/shard_map/ppermute | solution.py:438
  79.2 1.7 collective-permute-done.23
  81.8 2.9 %shard_map.51 = (f32[2,40,128]{2,1,0:T(8,128)S(1)}, f32[2,40,128]{2,1,0:T(8,128)S(1)}, f32[4,128]{1,0:T(4,128)S(1)}, f32[8,128]{1,0:T(8,128)S(1)}, f32[16,128]{1,0:T(8,128)S(1)}) custom-call(f32[16,4096]{1,0:T(8,128)S(1)} %copy-done.1, f32[16,4096]{1,0:T(8,128)S(1)} %collective-permute-done.2.refs_1_, f32[16,4096]{1,0:T(8,128)S(1)} %collective-permute-done.3.refs_2_, ...), custom_call_target="tpu_custom_call" | custom-call | flops 536870912 | bytes 1048576 | tf_op jit(solution)/shard_map/pallas_call | solution.py:421
  84.7 2.7 %collective-permute-start.24 = (f32[2,40,128]{2,1,0:T(8,128)S(1)}, f32[2,40,128]{2,1,0:T(8,128)S(1)}, u32[]{:S(2)}, u32[]{:S(2)}) collective-permute-start(f32[2,40,128]{2,1,0:T(8,128)S(1)} %get-tuple-element.47), channel_id=1, source_target_pairs={{0,24},{8,16},{16,8},{24,0},{1,25},{9,17},{17,9},{25,1},{2,26},{10... | collective-permute-start | bytes 122888 | tf_op jit(solution)/shard_map/ppermute | solution.py:438
  87.4 2.7 %collective-permute-done.24 = f32[2,40,128]{2,1,0:T(8,128)S(1)} collective-permute-done((f32[2,40,128]{2,1,0:T(8,128)S(1)}, f32[2,40,128]{2,1,0:T(8,128)S(1)}, u32[]{:S(2)}, u32[]{:S(2)}) %collective-permute-start.24) | collective-permute-done | bytes 40992 | tf_op jit(solution)/shard_map/ppermute | solution.py:438
  90.2 3.4 %collective-permute-done.25 = f32[40,128]{1,0:T(8,128)S(1)} collective-permute-done((f32[40,128]{1,0:T(8,128)S(1)}, f32[40,128]{1,0:T(8,128)S(1)}, u32[]{:S(2)}, u32[]{:S(2)}) %collective-permute-start.25) | collective-permute-done | bytes 20512 | tf_op jit(solution)/shard_map/ppermute | solution.py:438
  93.7 1.5 collective-permute-start.26
  95.2 1.5 collective-permute-done.26
  96.7 5.4 %collective-permute-start.27 = (f32[32,128]{1,0:T(8,128)S(1)}, f32[32,128]{1,0:T(8,128)S(1)}, u32[]{:S(2)}, u32[]{:S(2)}) collective-permute-start(f32[32,128]{1,0:T(8,128)S(1)} %slice_add_fusion), channel_id=1, source_target_pairs={{0,224},{32,64},{64,32},{96,128},{128,96},{160,192},{192,160},{224... | collective-permute-start | bytes 49160 | tf_op jit(solution)/shard_map/ppermute | solution.py:438
  102.2 1.5 collective-permute-done.27
  105.0 3.3 %collective-permute-done.28 = f32[32,128]{1,0:T(8,128)S(1)} collective-permute-done((f32[32,128]{1,0:T(8,128)S(1)}, f32[32,128]{1,0:T(8,128)S(1)}, u32[]{:S(2)}, u32[]{:S(2)}) %collective-permute-start.28) | collective-permute-done | bytes 16416 | tf_op jit(solution)/shard_map/ppermute | solution.py:438
  108.3 7.3 %all-gather.2.cloned.1.call-done.pack = f32[512,10880]{1,0:T(8,128)} async-done(((f32[16,10880]{1,0:T(8,128)}), f32[512,10880]{1,0:T(8,128)}) %all-gather.2.cloned.1.call-update) | async-done | bytes 22282256 | tf_op jit(solution)/shard_map/all_gather | solution.py:474
  115.6 3.7 %shard_map.52 = f32[32,128]{1,0:T(8,128)S(1)} custom-call(f32[512,10880]{1,0:T(8,128)} %all-gather.2.cloned.1.call-done.pack, f32[32,128]{1,0:T(8,128)S(1)} %add.100.summed), custom_call_target="tpu_custom_call" | custom-call | flops 536870912 | bytes 1048576 | tf_op jit(solution)/shard_map/pallas_call | solution.py:421
  119.3 1.3 collective-permute-start.29
  120.6 1.3 collective-permute-done.29
  122.0 3.0 %collective-permute-start.30 = (f32[32,128]{1,0:T(8,128)S(1)}, f32[32,128]{1,0:T(8,128)S(1)}, u32[]{:S(2)}, u32[]{:S(2)}) collective-permute-start(f32[32,128]{1,0:T(8,128)S(1)} %add.101), channel_id=1, source_target_pairs={{0,224},{32,64},{64,32},{96,128},{128,96},{160,192},{192,160},{224... | collective-permute-start | bytes 49160 | tf_op jit(solution)/shard_map/ppermute | solution.py:438
  126.1 2.9 %collective-permute-start.31 = (f32[32,128]{1,0:T(8,128)S(1)}, f32[32,128]{1,0:T(8,128)S(1)}, u32[]{:S(2)}, u32[]{:S(2)}) collective-permute-start(f32[32,128]{1,0:T(8,128)S(1)} %add.102), channel_id=1, source_target_pairs={{0,96},{32,192},{64,160},{96,0},{128,224},{160,64},{192,32},{224,1... | collective-permute-start | bytes 49160 | tf_op jit(solution)/shard_map/ppermute | solution.py:438
  129.0 1.5 collective-permute-done.31
  130.5 3.5 %shard_map.53 = f32[16,128]{1,0:T(8,128)S(1)} custom-call(f32[512,10880]{1,0:T(8,128)} %all-gather.2.cloned.1.call-done.pack, f32[16,128]{1,0:T(8,128)S(1)} %get-tuple-element.49.residual, f32[32,128]{1,0:T(8,128)S(1)} %add.103.rest_0_.s5), custom_call_target="tpu_custom_call" | custom-call | flops 536870912 | bytes 1048576 | tf_op jit(solution)/shard_map/pallas_call | solution.py:421
  135.1 1.4 collective-permute-done.32
  136.6 1.9 %collective-permute-start.33 = (f32[16,128]{1,0:T(8,128)S(1)}, f32[16,128]{1,0:T(8,128)S(1)}, u32[]{:S(2)}, u32[]{:S(2)}) collective-permute-start(f32[16,128]{1,0:T(8,128)S(1)} %add.104), channel_id=1, source_target_pairs={{0,64},{32,96},{64,0},{96,32},{128,192},{160,224},{192,128},{224,1... | collective-permute-start | bytes 24584 | tf_op jit(solution)/shard_map/ppermute | solution.py:438
  138.5 1.4 collective-permute-done.33
  140.0 2.9 %shard_map.54 = f32[8,128]{1,0:T(8,128)S(1)} custom-call(f32[512,10880]{1,0:T(8,128)} %all-gather.2.cloned.1.call-done.pack, f32[8,128]{1,0:T(8,128)S(1)} %get-tuple-element.50.residual, f32[32,128]{1,0:T(8,128)S(1)} %add.103.rest_0_.s5, f32[16,128]{1,0:T(8,128)S(1)} %add.105.rest_1_.s4), custom_call_target="tpu_custom_call" | custom-call | flops 536870912 | bytes 1048576 | tf_op jit(solution)/shard_map/pallas_call | solution.py:421
  145.4 6.0 %shard_map.55 = f32[16,128]{1,0:T(8,128)S(1)} custom-call(f32[512,10880]{1,0:T(8,128)} %all-gather.2.cloned.1.call-done.pack, f32[8,128]{1,0:T(8,128)S(1)} %slice.30.r01, f32[4,128]{1,0:T(4,128)S(1)} %get-tuple-element.48.r2, f32[32,128]{1,0:T(8,128)S(1)} %add.103.rest_0_.s5, f32[16,128]{1,0:T(8,128)S(1)} %add.105.rest_1_.s4, f32[8,128]{1,0:T(8,128)S(1)} %add.106.s3), custom_call_target="tpu_custom_call" | custom-call | flops 536870912 | bytes 1048576 | tf_op jit(solution)/shard_map/pallas_call | solution.py:421
  151.9 22.4 %all_to_all.5 = f32[32,6,16]{2,1,0:T(8,128)S(1)} all-to-all(f32[32,6,16]{2,1,0:T(8,128)S(1)} %copy.8), channel_id=1, replica_groups=mesh['z'=8,'x'=4,'blk'=8] {'x','blk'}, dimensions={0} | all-to-all | bytes 24576 | tf_op jit(solution)/shard_map/all_to_all | solution.py:556
  (90 shorter events, 23.5 us)
Async XLA Ops:
  6.5 109.0 %all-gather.2.cloned.1.call-start = ((), (), s32[]{:S(2)}) async-start(), calls=%async_computation.1 | async-start | bytes 22978560 | tf_op jit(solution)/shard_map/all_gather | solution.py:474
  9.8 7.6 %collective-permute-start = (f32[16,2944]{1,0:T(8,128)}, f32[16,2944]{1,0:T(8,128)S(1)}, u32[]{:S(2)}, u32[]{:S(2)}) collective-permute-start(f32[16,2944]{1,0:T(8,128)} %get-tuple-element.30.refs_0_), channel_id=1, source_target_pairs={{0,4},{1,5},{2,6},{3,7},{4,0},{5,1},{6,2},{7,3},{8,12},{9,13},{10,... | collective-permute-start | bytes 565256 | tf_op jit(solution)/shard_map/ppermute | solution.py:438
  13.7 9.3 %collective-permute-start.5 = (f32[16,2944]{1,0:T(8,128)}, f32[16,2944]{1,0:T(8,128)S(1)}, u32[]{:S(2)}, u32[]{:S(2)}) collective-permute-start(f32[16,2944]{1,0:T(8,128)} %get-tuple-element.30.refs_0_), channel_id=1, source_target_pairs={{0,2},{1,3},{2,4},{3,5},{4,6},{5,7},{6,0},{7,1},{8,10},{9,11},{10,... | collective-permute-start | bytes 565256 | tf_op jit(solution)/shard_map/ppermute | solution.py:438
  14.1 10.2 %collective-permute-start.6 = (f32[16,2944]{1,0:T(8,128)}, f32[16,2944]{1,0:T(8,128)S(1)}, u32[]{:S(2)}, u32[]{:S(2)}) collective-permute-start(f32[16,2944]{1,0:T(8,128)} %get-tuple-element.30.refs_0_), channel_id=1, source_target_pairs={{0,6},{1,7},{2,0},{3,1},{4,2},{5,3},{6,4},{7,5},{8,14},{9,15},{10,... | collective-permute-start | bytes 565256 | tf_op jit(solution)/shard_map/ppermute | solution.py:438
  17.5 6.8 %collective-permute-start.1 = (f32[16,2944]{1,0:T(8,128)S(1)}, f32[16,2944]{1,0:T(8,128)S(1)}, u32[]{:S(2)}, u32[]{:S(2)}) collective-permute-start(f32[16,2944]{1,0:T(8,128)S(1)} %collective-permute-done.refs_3_), channel_id=1, source_target_pairs={{0,1},{1,0},{2,3},{3,2},{4,5},{5,4},{6,7},{7,6},{8,9},{9,8},{10,11... | collective-permute-start | bytes 565256 | tf_op jit(solution)/shard_map/ppermute | solution.py:438
  21.7 5.3 %collective-permute-start.7 = (f32[16,2944]{1,0:T(8,128)}, f32[16,2944]{1,0:T(8,128)S(1)}, u32[]{:S(2)}, u32[]{:S(2)}) collective-permute-start(f32[16,2944]{1,0:T(8,128)} %get-tuple-element.30.refs_0_), channel_id=1, source_target_pairs={{0,1},{1,0},{2,3},{3,2},{4,5},{5,4},{6,7},{7,6},{8,9},{9,8},{10,11... | collective-permute-start | bytes 565256 | tf_op jit(solution)/shard_map/ppermute | solution.py:438
  22.9 4.7 %collective-permute-start.8 = (f32[16,2944]{1,0:T(8,128)S(1)}, f32[16,2944]{1,0:T(8,128)S(1)}, u32[]{:S(2)}, u32[]{:S(2)}) collective-permute-start(f32[16,2944]{1,0:T(8,128)S(1)} %collective-permute-done.5.refs_1_), channel_id=1, source_target_pairs={{0,1},{1,0},{2,3},{3,2},{4,5},{5,4},{6,7},{7,6},{8,9},{9,8},{10,11... | collective-permute-start | bytes 565256 | tf_op jit(solution)/shard_map/ppermute | solution.py:438
  24.3 3.4 %collective-permute-start.9 = (f32[16,2944]{1,0:T(8,128)S(1)}, f32[16,2944]{1,0:T(8,128)S(1)}, u32[]{:S(2)}, u32[]{:S(2)}) collective-permute-start(f32[16,2944]{1,0:T(8,128)S(1)} %collective-permute-done.6.refs_2_), channel_id=1, source_target_pairs={{0,1},{1,0},{2,3},{3,2},{4,5},{5,4},{6,7},{7,6},{8,9},{9,8},{10,11... | collective-permute-start | bytes 565256 | tf_op jit(solution)/shard_map/ppermute | solution.py:438
  24.3 23.1 %collective-permute-start.2 = (f32[16,4096]{1,0:T(8,128)}, f32[16,4096]{1,0:T(8,128)S(1)}, u32[]{:S(2)}, u32[]{:S(2)}) collective-permute-start(f32[16,4096]{1,0:T(8,128)} %get-tuple-element.38.refs_0_), channel_id=1, source_target_pairs={{0,2},{1,3},{2,4},{3,5},{4,6},{5,7},{6,0},{7,1},{8,10},{9,11},{10,... | collective-permute-start | bytes 786440 | tf_op jit(solution)/shard_map/ppermute | solution.py:438
  25.2 22.2 %collective-permute-start.3 = (f32[16,4096]{1,0:T(8,128)}, f32[16,4096]{1,0:T(8,128)S(1)}, u32[]{:S(2)}, u32[]{:S(2)}) collective-permute-start(f32[16,4096]{1,0:T(8,128)} %get-tuple-element.38.refs_0_), channel_id=1, source_target_pairs={{0,6},{1,7},{2,0},{3,1},{4,2},{5,3},{6,4},{7,5},{8,14},{9,15},{10,... | collective-permute-start | bytes 786440 | tf_op jit(solution)/shard_map/ppermute | solution.py:438
  27.0 21.3 %collective-permute-start.4 = (f32[16,4096]{1,0:T(8,128)}, f32[16,4096]{1,0:T(8,128)S(1)}, u32[]{:S(2)}, u32[]{:S(2)}) collective-permute-start(f32[16,4096]{1,0:T(8,128)} %get-tuple-element.38.refs_0_), channel_id=1, source_target_pairs={{0,4},{1,5},{2,6},{3,7},{4,0},{5,1},{6,2},{7,3},{8,12},{9,13},{10,... | collective-permute-start | bytes 786440 | tf_op jit(solution)/shard_map/ppermute | solution.py:438
  27.7 1.0 copy-start.2
  31.6 2.9 %collective-permute-start.10 = (f32[8,128]{1,0:T(8,128)S(1)}, f32[8,128]{1,0:T(8,128)S(1)}, u32[]{:S(2)}, u32[]{:S(2)}) collective-permute-start(f32[8,128]{1,0:T(8,128)S(1)} %get-tuple-element.33), channel_id=1, source_target_pairs={{0,8},{8,0},{16,24},{24,16},{1,9},{9,1},{17,25},{25,17},{2,10},{10... | collective-permute-start | bytes 12296 | tf_op jit(solution)/shard_map/ppermute | solution.py:438
  34.5 0.9 copy-start.3
  37.4 3.0 %collective-permute-start.11 = (f32[16,128]{1,0:T(8,128)S(1)}, f32[16,128]{1,0:T(8,128)S(1)}, u32[]{:S(2)}, u32[]{:S(2)}) collective-permute-start(f32[16,128]{1,0:T(8,128)S(1)} %get-tuple-element.35), channel_id=1, source_target_pairs={{0,8},{8,0},{16,24},{24,16},{1,9},{9,1},{17,25},{25,17},{2,10},{10... | collective-permute-start | bytes 24584 | tf_op jit(solution)/shard_map/ppermute | solution.py:438
  40.4 4.1 %collective-permute-start.12 = (f32[16,128]{1,0:T(8,128)S(1)}, f32[16,128]{1,0:T(8,128)S(1)}, u32[]{:S(2)}, u32[]{:S(2)}) collective-permute-start(f32[16,128]{1,0:T(8,128)S(1)} %add.87), channel_id=1, source_target_pairs={{0,24},{8,16},{16,8},{24,0},{1,25},{9,17},{17,9},{25,1},{2,26},{10... | collective-permute-start | bytes 24584 | tf_op jit(solution)/shard_map/ppermute | solution.py:438
  44.5 0.9 copy-start.4
  48.3 12.4 %collective-permute-start.13 = (f32[16,4096]{1,0:T(8,128)}, f32[16,4096]{1,0:T(8,128)S(1)}, u32[]{:S(2)}, u32[]{:S(2)}) collective-permute-start(f32[16,4096]{1,0:T(8,128)} %get-tuple-element.38.refs_0_), channel_id=1, source_target_pairs={{0,1},{1,0},{2,3},{3,2},{4,5},{5,4},{6,7},{7,6},{8,9},{9,8},{10,11... | collective-permute-start | bytes 786440 | tf_op jit(solution)/shard_map/ppermute | solution.py:438
  50.8 9.9 %collective-permute-start.14 = (f32[16,4096]{1,0:T(8,128)S(1)}, f32[16,4096]{1,0:T(8,128)S(1)}, u32[]{:S(2)}, u32[]{:S(2)}) collective-permute-start(f32[16,4096]{1,0:T(8,128)S(1)} %collective-permute-done.2.refs_1_), channel_id=1, source_target_pairs={{0,1},{1,0},{2,3},{3,2},{4,5},{5,4},{6,7},{7,6},{8,9},{9,8},{10,11... | collective-permute-start | bytes 786440 | tf_op jit(solution)/shard_map/ppermute | solution.py:438
  50.9 9.8 %collective-permute-start.15 = (f32[16,4096]{1,0:T(8,128)S(1)}, f32[16,4096]{1,0:T(8,128)S(1)}, u32[]{:S(2)}, u32[]{:S(2)}) collective-permute-start(f32[16,4096]{1,0:T(8,128)S(1)} %collective-permute-done.3.refs_2_), channel_id=1, source_target_pairs={{0,1},{1,0},{2,3},{3,2},{4,5},{5,4},{6,7},{7,6},{8,9},{9,8},{10,11... | collective-permute-start | bytes 786440 | tf_op jit(solution)/shard_map/ppermute | solution.py:438
  51.3 9.4 %collective-permute-start.16 = (f32[16,4096]{1,0:T(8,128)S(1)}, f32[16,4096]{1,0:T(8,128)S(1)}, u32[]{:S(2)}, u32[]{:S(2)}) collective-permute-start(f32[16,4096]{1,0:T(8,128)S(1)} %collective-permute-done.4.refs_3_), channel_id=1, source_target_pairs={{0,1},{1,0},{2,3},{3,2},{4,5},{5,4},{6,7},{7,6},{8,9},{9,8},{10,11... | collective-permute-start | bytes 786440 | tf_op jit(solution)/shard_map/ppermute | solution.py:438
  51.4 2.6 %collective-permute-start.17 = (f32[32,128]{1,0:T(8,128)S(1)}, f32[32,128]{1,0:T(8,128)S(1)}, u32[]{:S(2)}, u32[]{:S(2)}) collective-permute-start(f32[32,128]{1,0:T(8,128)S(1)} %get-tuple-element.37), channel_id=1, source_target_pairs={{0,8},{8,0},{16,24},{24,16},{1,9},{9,1},{17,25},{25,17},{2,10},{10... | collective-permute-start | bytes 49160 | tf_op jit(solution)/shard_map/ppermute | solution.py:438
  54.0 3.8 %collective-permute-start.18 = (f32[32,128]{1,0:T(8,128)S(1)}, f32[32,128]{1,0:T(8,128)S(1)}, u32[]{:S(2)}, u32[]{:S(2)}) collective-permute-start(f32[32,128]{1,0:T(8,128)S(1)} %add.89), channel_id=1, source_target_pairs={{0,24},{8,16},{16,8},{24,0},{1,25},{9,17},{17,9},{25,1},{2,26},{10... | collective-permute-start | bytes 49160 | tf_op jit(solution)/shard_map/ppermute | solution.py:438
  57.8 2.9 %collective-permute-start.19 = (f32[32,128]{1,0:T(8,128)S(1)}, f32[32,128]{1,0:T(8,128)S(1)}, u32[]{:S(2)}, u32[]{:S(2)}) collective-permute-start(f32[32,128]{1,0:T(8,128)S(1)} %add.90), channel_id=1, source_target_pairs={{0,32},{32,0},{64,96},{96,64},{128,160},{160,128},{192,224},{224,1... | collective-permute-start | bytes 49160 | tf_op jit(solution)/shard_map/ppermute | solution.py:438
  60.7 1.0 copy-start
  63.9 3.6 %collective-permute-start.20 = (f32[64,128]{1,0:T(8,128)S(1)}, f32[64,128]{1,0:T(8,128)S(1)}, u32[]{:S(2)}, u32[]{:S(2)}) collective-permute-start(f32[64,128]{1,0:T(8,128)S(1)} %get-tuple-element.44), channel_id=1, source_target_pairs={{0,8},{8,0},{16,24},{24,16},{1,9},{9,1},{17,25},{25,17},{2,10},{10... | collective-permute-start | bytes 98312 | tf_op jit(solution)/shard_map/ppermute | solution.py:438
  67.5 5.0 %collective-permute-start.21 = (f32[64,128]{1,0:T(8,128)S(1)}, f32[64,128]{1,0:T(8,128)S(1)}, u32[]{:S(2)}, u32[]{:S(2)}) collective-permute-start(f32[64,128]{1,0:T(8,128)S(1)} %add.92), channel_id=1, source_target_pairs={{0,24},{8,16},{16,8},{24,0},{1,25},{9,17},{17,9},{25,1},{2,26},{10... | collective-permute-start | bytes 98312 | tf_op jit(solution)/shard_map/ppermute | solution.py:438
  72.5 3.2 %collective-permute-start.22 = (f32[64,128]{1,0:T(8,128)S(1)}, f32[64,128]{1,0:T(8,128)S(1)}, u32[]{:S(2)}, u32[]{:S(2)}) collective-permute-start(f32[64,128]{1,0:T(8,128)S(1)} %add.93), channel_id=1, source_target_pairs={{0,32},{32,0},{64,96},{96,64},{128,160},{160,128},{192,224},{224,1... | collective-permute-start | bytes 98312 | tf_op jit(solution)/shard_map/ppermute | solution.py:438
  75.8 5.1 %collective-permute-start.23 = (f32[64,128]{1,0:T(8,128)S(1)}, f32[64,128]{1,0:T(8,128)S(1)}, u32[]{:S(2)}, u32[]{:S(2)}) collective-permute-start(f32[64,128]{1,0:T(8,128)S(1)} %add.94), channel_id=1, source_target_pairs={{0,64},{32,96},{64,0},{96,32},{128,192},{160,224},{192,128},{224,1... | collective-permute-start | bytes 98312 | tf_op jit(solution)/shard_map/ppermute | solution.py:438
  80.9 1.0 copy-start.1
  84.7 5.4 %collective-permute-start.24 = (f32[2,40,128]{2,1,0:T(8,128)S(1)}, f32[2,40,128]{2,1,0:T(8,128)S(1)}, u32[]{:S(2)}, u32[]{:S(2)}) collective-permute-start(f32[2,40,128]{2,1,0:T(8,128)S(1)} %get-tuple-element.47), channel_id=1, source_target_pairs={{0,24},{8,16},{16,8},{24,0},{1,25},{9,17},{17,9},{25,1},{2,26},{10... | collective-permute-start | bytes 122888 | tf_op jit(solution)/shard_map/ppermute | solution.py:438
  90.1 3.5 %collective-permute-start.25 = (f32[40,128]{1,0:T(8,128)S(1)}, f32[40,128]{1,0:T(8,128)S(1)}, u32[]{:S(2)}, u32[]{:S(2)}) collective-permute-start(f32[40,128]{1,0:T(8,128)S(1)} %slice_bitcast_fusion), channel_id=1, source_target_pairs={{0,8},{8,0},{16,24},{24,16},{1,9},{9,1},{17,25},{25,17},{2,10},{10... | collective-permute-start | bytes 61448 | tf_op jit(solution)/shard_map/ppermute | solution.py:438
  93.7 3.1 %collective-permute-start.26 = (f32[32,128]{1,0:T(8,128)S(1)}, f32[32,128]{1,0:T(8,128)S(1)}, u32[]{:S(2)}, u32[]{:S(2)}) collective-permute-start(f32[32,128]{1,0:T(8,128)S(1)} %slice.31), channel_id=1, source_target_pairs={{0,32},{32,0},{64,96},{96,64},{128,160},{160,128},{192,224},{224,1... | collective-permute-start | bytes 49160 | tf_op jit(solution)/shard_map/ppermute | solution.py:438
  96.7 7.0 %collective-permute-start.27 = (f32[32,128]{1,0:T(8,128)S(1)}, f32[32,128]{1,0:T(8,128)S(1)}, u32[]{:S(2)}, u32[]{:S(2)}) collective-permute-start(f32[32,128]{1,0:T(8,128)S(1)} %slice_add_fusion), channel_id=1, source_target_pairs={{0,224},{32,64},{64,32},{96,128},{128,96},{160,192},{192,160},{224... | collective-permute-start | bytes 49160 | tf_op jit(solution)/shard_map/ppermute | solution.py:438
  103.7 4.6 %collective-permute-start.28 = (f32[32,128]{1,0:T(8,128)S(1)}, f32[32,128]{1,0:T(8,128)S(1)}, u32[]{:S(2)}, u32[]{:S(2)}) collective-permute-start(f32[32,128]{1,0:T(8,128)S(1)} %add.99), channel_id=1, source_target_pairs={{0,96},{32,192},{64,160},{96,0},{128,224},{160,64},{192,32},{224,1... | collective-permute-start | bytes 49160 | tf_op jit(solution)/shard_map/ppermute | solution.py:438
  119.3 2.7 %collective-permute-start.29 = (f32[32,128]{1,0:T(8,128)S(1)}, f32[32,128]{1,0:T(8,128)S(1)}, u32[]{:S(2)}, u32[]{:S(2)}) collective-permute-start(f32[32,128]{1,0:T(8,128)S(1)} %shard_map.52), channel_id=1, source_target_pairs={{0,32},{32,0},{64,96},{96,64},{128,160},{160,128},{192,224},{224,1... | collective-permute-start | bytes 49160 | tf_op jit(solution)/shard_map/ppermute | solution.py:438
  122.0 4.1 %collective-permute-start.30 = (f32[32,128]{1,0:T(8,128)S(1)}, f32[32,128]{1,0:T(8,128)S(1)}, u32[]{:S(2)}, u32[]{:S(2)}) collective-permute-start(f32[32,128]{1,0:T(8,128)S(1)} %add.101), channel_id=1, source_target_pairs={{0,224},{32,64},{64,32},{96,128},{128,96},{160,192},{192,160},{224... | collective-permute-start | bytes 49160 | tf_op jit(solution)/shard_map/ppermute | solution.py:438
  126.1 4.4 %collective-permute-start.31 = (f32[32,128]{1,0:T(8,128)S(1)}, f32[32,128]{1,0:T(8,128)S(1)}, u32[]{:S(2)}, u32[]{:S(2)}) collective-permute-start(f32[32,128]{1,0:T(8,128)S(1)} %add.102), channel_id=1, source_target_pairs={{0,96},{32,192},{64,160},{96,0},{128,224},{160,64},{192,32},{224,1... | collective-permute-start | bytes 49160 | tf_op jit(solution)/shard_map/ppermute | solution.py:438
  134.0 2.6 %collective-permute-start.32 = (f32[16,128]{1,0:T(8,128)S(1)}, f32[16,128]{1,0:T(8,128)S(1)}, u32[]{:S(2)}, u32[]{:S(2)}) collective-permute-start(f32[16,128]{1,0:T(8,128)S(1)} %shard_map.53), channel_id=1, source_target_pairs={{0,32},{32,0},{64,96},{96,64},{128,160},{160,128},{192,224},{224,1... | collective-permute-start | bytes 24584 | tf_op jit(solution)/shard_map/ppermute | solution.py:438
  136.6 3.4 %collective-permute-start.33 = (f32[16,128]{1,0:T(8,128)S(1)}, f32[16,128]{1,0:T(8,128)S(1)}, u32[]{:S(2)}, u32[]{:S(2)}) collective-permute-start(f32[16,128]{1,0:T(8,128)S(1)} %add.104), channel_id=1, source_target_pairs={{0,64},{32,96},{64,0},{96,32},{128,192},{160,224},{192,128},{224,1... | collective-permute-start | bytes 24584 | tf_op jit(solution)/shard_map/ppermute | solution.py:438
  142.8 2.5 %collective-permute-start.34 = (f32[8,128]{1,0:T(8,128)S(1)}, f32[8,128]{1,0:T(8,128)S(1)}, u32[]{:S(2)}, u32[]{:S(2)}) collective-permute-start(f32[8,128]{1,0:T(8,128)S(1)} %shard_map.54), channel_id=1, source_target_pairs={{0,32},{32,0},{64,96},{96,64},{128,160},{160,128},{192,224},{224,1... | collective-permute-start | bytes 12296 | tf_op jit(solution)/shard_map/ppermute | solution.py:438
Sparse Core Ops, SparseCore 0:
  10.0 105.5 all-gather.1

commit v3 on v2

--- a/solution.py
+++ b/solution.py
@@ -223,7 +223,7 @@
         )
         return carry
 
-    lax.fori_loop(0, SLOTS, slot, 0, unroll=4)
+    lax.fori_loop(0, SLOTS, slot, 0, unroll=8)
 
 
 def path_update(level, before, total, path, ahead):

time: 182 us -> 181 us (level)
  transfers between devices with their start and end apart: 36 -> 36, of which waited for: 25 -> 25; matrix products, arithmetic and copies ran while one was open for 0% -> 0% of each run, Pallas kernels for 7% -> 6%
where the time goes in v3:
time: 181 us
  starting transfers between devices  59 us (33%)
  waiting for transfers between devices  50.8 us (28%)
  Pallas kernels  29.7 us (16%)
  blocking collectives  21.4 us (12%)
  between operations  13.7 us (8%)
  local copies, waits for them, and re-layouts  6.1 us (3%)
    ppermute x35, starting transfers between devices, moved(): return lax.ppermute(value, axis, [(i, to(i)) for i in range(size)])  59 us
    ppermute x35, waiting for transfers between devices, moved(): return lax.ppermute(value, axis, [(i, to(i)) for i in range(size)])  43 us
    pallas_call x9, Pallas kernels, call(): pl.pallas_call(body, out_shape=outs, in_specs=specs, out_specs=jax.tree.m...  26.5 us
    all_to_all x1, blocking collectives, local(): out = lax.all_to_all(jnp.transpose(out, (1, 0, 2)), PLANE, 0, 0)  21.4 us
    all_gather x1, waiting for transfers between devices, local(): pack = lax.all_gather(pack, PLANE, axis=0, tiled=True)  7.81 us
    unnamed x15, local copies, waits for them, and re-layouts  4.76 us
  transfers between devices with their start and end apart: 36, of which 25 were waited for; matrix products, arithmetic and copies ran while one was open for 0% of the time, Pallas kernels for 6%

profile of v3, /device:TPU:1, one launch (start us, length us, event | category | flops | bytes accessed | tf_op | source)
XLA Modules:
  0.0 181.0 jit_solution(14179594847275949956)
XLA Ops:
  6.5 3.3 %shard_map.46 = (f32[16,10880]{1,0:T(8,128)}, f32[16,2944]{1,0:T(8,128)}, f32[16,4096]{1,0:T(8,128)}) custom-call(f32[6,16,32]{2,1,0:T(8,128)} %bitcast.18, s32[5,1,512]{2,1,0:T(1,128)} %rows_index.1, f32[16,8064]{1,0:T(8,128)} %diag_inverse.1, f32[5,16,512]{2,1,0:T(8,128)} %off_diagonal.1), custom_call_target="tpu_custom_call" | custom-call | tf_op jit(solution)/shard_map/pallas_call | solution.py:466
  9.8 3.8 %collective-permute-start = (f32[16,2944]{1,0:T(8,128)}, f32[16,2944]{1,0:T(8,128)S(1)}, u32[]{:S(2)}, u32[]{:S(2)}) collective-permute-start(f32[16,2944]{1,0:T(8,128)} %get-tuple-element.30.refs_0_), channel_id=1, source_target_pairs={{0,4},{1,5},{2,6},{3,7},{4,0},{5,1},{6,2},{7,3},{8,12},{9,13},{10,... | collective-permute-start | bytes 565256 | tf_op jit(solution)/shard_map/ppermute | solution.py:438
  14.1 2.3 %collective-permute-start.6 = (f32[16,2944]{1,0:T(8,128)}, f32[16,2944]{1,0:T(8,128)S(1)}, u32[]{:S(2)}, u32[]{:S(2)}) collective-permute-start(f32[16,2944]{1,0:T(8,128)} %get-tuple-element.30.refs_0_), channel_id=1, source_target_pairs={{0,6},{1,7},{2,0},{3,1},{4,2},{5,3},{6,4},{7,5},{8,14},{9,15},{10,... | collective-permute-start | bytes 565256 | tf_op jit(solution)/shard_map/ppermute | solution.py:438
  17.5 4.2 %collective-permute-start.1 = (f32[16,2944]{1,0:T(8,128)S(1)}, f32[16,2944]{1,0:T(8,128)S(1)}, u32[]{:S(2)}, u32[]{:S(2)}) collective-permute-start(f32[16,2944]{1,0:T(8,128)S(1)} %collective-permute-done.refs_3_), channel_id=1, source_target_pairs={{0,1},{1,0},{2,3},{3,2},{4,5},{5,4},{6,7},{7,6},{8,9},{9,8},{10,11... | collective-permute-start | bytes 565256 | tf_op jit(solution)/shard_map/ppermute | solution.py:438
  25.2 1.8 %collective-permute-start.3 = (f32[16,4096]{1,0:T(8,128)}, f32[16,4096]{1,0:T(8,128)S(1)}, u32[]{:S(2)}, u32[]{:S(2)}) collective-permute-start(f32[16,4096]{1,0:T(8,128)} %get-tuple-element.38.refs_0_), channel_id=1, source_target_pairs={{0,6},{1,7},{2,0},{3,1},{4,2},{5,3},{6,4},{7,5},{8,14},{9,15},{10,... | collective-permute-start | bytes 786440 | tf_op jit(solution)/shard_map/ppermute | solution.py:438
  28.6 2.8 %shard_map.47 = (f32[256,128]{1,0:T(8,128)S(1)}, f32[8,128]{1,0:T(8,128)S(1)}, f32[4,128]{1,0:T(4,128)S(1)}, s32[5,8,512]{2,1,0:T(8,128)S(1)}) custom-call(f32[16,2944]{1,0:T(8,128)S(1)} %copy-done.2, f32[16,2944]{1,0:T(8,128)S(1)} %collective-permute-done.5.refs_1_, f32[16,2944]{1,0:T(8,128)S(1)} %collective-permute-done.6.refs_2_, ...), custom_call_target="tpu_custom_call" | custom-call | flops 536870912 | bytes 1048576 | tf_op jit(solution)/shard_map/pallas_call | solution.py:421
  32.7 1.7 collective-permute-done.10
  35.3 1.6 shard_map.48
  38.2 1.7 collective-permute-done.11
  39.9 2.5 %collective-permute-start.12 = (f32[16,128]{1,0:T(8,128)S(1)}, f32[16,128]{1,0:T(8,128)S(1)}, u32[]{:S(2)}, u32[]{:S(2)}) collective-permute-start(f32[16,128]{1,0:T(8,128)S(1)} %add.87), channel_id=1, source_target_pairs={{0,24},{8,16},{16,8},{24,0},{1,25},{9,17},{17,9},{25,1},{2,26},{10... | collective-permute-start | bytes 24584 | tf_op jit(solution)/shard_map/ppermute | solution.py:438
  42.4 1.7 collective-permute-done.12
  45.1 1.7 shard_map.49
  46.8 1.5 collective-permute-done.4.refs_3_
  48.3 1.9 %collective-permute-start.13 = (f32[16,4096]{1,0:T(8,128)}, f32[16,4096]{1,0:T(8,128)S(1)}, u32[]{:S(2)}, u32[]{:S(2)}) collective-permute-start(f32[16,4096]{1,0:T(8,128)} %get-tuple-element.38.refs_0_), channel_id=1, source_target_pairs={{0,1},{1,0},{2,3},{3,2},{4,5},{5,4},{6,7},{7,6},{8,9},{9,8},{10,11... | collective-permute-start | bytes 786440 | tf_op jit(solution)/shard_map/ppermute | solution.py:438
  51.6 1.8 %collective-permute-done.17 = f32[32,128]{1,0:T(8,128)S(1)} collective-permute-done((f32[32,128]{1,0:T(8,128)S(1)}, f32[32,128]{1,0:T(8,128)S(1)}, u32[]{:S(2)}, u32[]{:S(2)}) %collective-permute-start.17) | collective-permute-done | bytes 16416 | tf_op jit(solution)/shard_map/ppermute | solution.py:438
  53.4 2.5 %collective-permute-start.18 = (f32[32,128]{1,0:T(8,128)S(1)}, f32[32,128]{1,0:T(8,128)S(1)}, u32[]{:S(2)}, u32[]{:S(2)}) collective-permute-start(f32[32,128]{1,0:T(8,128)S(1)} %add.89), channel_id=1, source_target_pairs={{0,24},{8,16},{16,8},{24,0},{1,25},{9,17},{17,9},{25,1},{2,26},{10... | collective-permute-start | bytes 49160 | tf_op jit(solution)/shard_map/ppermute | solution.py:438
  57.2 1.6 collective-permute-start.19
  61.0 1.9 %shard_map.50 = (f32[256,128]{1,0:T(8,128)S(1)}, f32[64,128]{1,0:T(8,128)S(1)}) custom-call(f32[16,4096]{1,0:T(8,128)S(1)} %copy-done, f32[16,4096]{1,0:T(8,128)S(1)} %collective-permute-done.2.refs_1_, f32[16,4096]{1,0:T(8,128)S(1)} %collective-permute-done.3.refs_2_, f32[16,4096]{1,0:T(8,128)S(1)} %collective-permute-done.4.refs_3_, ...), custom_call_target="tpu_custom_call" | custom-call | flops 536870912 | bytes 1048576 | tf_op jit(solution)/shard_map/pallas_call | solution.py:421
  63.0 2.9 %collective-permute-done.20 = f32[64,128]{1,0:T(8,128)S(1)} collective-permute-done((f32[64,128]{1,0:T(8,128)S(1)}, f32[64,128]{1,0:T(8,128)S(1)}, u32[]{:S(2)}, u32[]{:S(2)}) %collective-permute-start.20) | collective-permute-done | bytes 32800 | tf_op jit(solution)/shard_map/ppermute | solution.py:438
  65.9 3.1 %collective-permute-start.21 = (f32[64,128]{1,0:T(8,128)S(1)}, f32[64,128]{1,0:T(8,128)S(1)}, u32[]{:S(2)}, u32[]{:S(2)}) collective-permute-start(f32[64,128]{1,0:T(8,128)S(1)} %add.92), channel_id=1, source_target_pairs={{0,24},{8,16},{16,8},{24,0},{1,25},{9,17},{17,9},{25,1},{2,26},{10... | collective-permute-start | bytes 98312 | tf_op jit(solution)/shard_map/ppermute | solution.py:438
  69.0 2.4 %collective-permute-done.21 = f32[64,128]{1,0:T(8,128)S(1)} collective-permute-done((f32[64,128]{1,0:T(8,128)S(1)}, f32[64,128]{1,0:T(8,128)S(1)}, u32[]{:S(2)}, u32[]{:S(2)}) %collective-permute-start.21) | collective-permute-done | bytes 32800 | tf_op jit(solution)/shard_map/ppermute | solution.py:438
  71.4 1.9 %collective-permute-start.22 = (f32[64,128]{1,0:T(8,128)S(1)}, f32[64,128]{1,0:T(8,128)S(1)}, u32[]{:S(2)}, u32[]{:S(2)}) collective-permute-start(f32[64,128]{1,0:T(8,128)S(1)} %add.93), channel_id=1, source_target_pairs={{0,32},{32,0},{64,96},{96,64},{128,160},{160,128},{192,224},{224,1... | collective-permute-start | bytes 98312 | tf_op jit(solution)/shard_map/ppermute | solution.py:438
  73.3 1.7 collective-permute-done.22
  75.0 3.7 %collective-permute-start.23 = (f32[64,128]{1,0:T(8,128)S(1)}, f32[64,128]{1,0:T(8,128)S(1)}, u32[]{:S(2)}, u32[]{:S(2)}) collective-permute-start(f32[64,128]{1,0:T(8,128)S(1)} %add.94), channel_id=1, source_target_pairs={{0,64},{32,96},{64,0},{96,32},{128,192},{160,224},{192,128},{224,1... | collective-permute-start | bytes 98312 | tf_op jit(solution)/shard_map/ppermute | solution.py:438
  78.7 1.7 collective-permute-done.23
  81.4 2.4 %shard_map.51 = (f32[2,40,128]{2,1,0:T(8,128)S(1)}, f32[2,40,128]{2,1,0:T(8,128)S(1)}, f32[4,128]{1,0:T(4,128)S(1)}, f32[8,128]{1,0:T(8,128)S(1)}, f32[16,128]{1,0:T(8,128)S(1)}) custom-call(f32[16,4096]{1,0:T(8,128)S(1)} %copy-done.1, f32[16,4096]{1,0:T(8,128)S(1)} %collective-permute-done.2.refs_1_, f32[16,4096]{1,0:T(8,128)S(1)} %collective-permute-done.3.refs_2_, ...), custom_call_target="tpu_custom_call" | custom-call | flops 536870912 | bytes 1048576 | tf_op jit(solution)/shard_map/pallas_call | solution.py:421
  83.8 2.7 %collective-permute-start.24 = (f32[2,40,128]{2,1,0:T(8,128)S(1)}, f32[2,40,128]{2,1,0:T(8,128)S(1)}, u32[]{:S(2)}, u32[]{:S(2)}) collective-permute-start(f32[2,40,128]{2,1,0:T(8,128)S(1)} %get-tuple-element.47), channel_id=1, source_target_pairs={{0,24},{8,16},{16,8},{24,0},{1,25},{9,17},{17,9},{25,1},{2,26},{10... | collective-permute-start | bytes 122888 | tf_op jit(solution)/shard_map/ppermute | solution.py:438
  86.6 2.6 %collective-permute-done.24 = f32[2,40,128]{2,1,0:T(8,128)S(1)} collective-permute-done((f32[2,40,128]{2,1,0:T(8,128)S(1)}, f32[2,40,128]{2,1,0:T(8,128)S(1)}, u32[]{:S(2)}, u32[]{:S(2)}) %collective-permute-start.24) | collective-permute-done | bytes 40992 | tf_op jit(solution)/shard_map/ppermute | solution.py:438
  89.4 3.4 %collective-permute-done.25 = f32[40,128]{1,0:T(8,128)S(1)} collective-permute-done((f32[40,128]{1,0:T(8,128)S(1)}, f32[40,128]{1,0:T(8,128)S(1)}, u32[]{:S(2)}, u32[]{:S(2)}) %collective-permute-start.25) | collective-permute-done | bytes 20512 | tf_op jit(solution)/shard_map/ppermute | solution.py:438
  92.8 1.5 collective-permute-start.26
  94.3 1.5 collective-permute-done.26
  95.9 5.6 %collective-permute-start.27 = (f32[32,128]{1,0:T(8,128)S(1)}, f32[32,128]{1,0:T(8,128)S(1)}, u32[]{:S(2)}, u32[]{:S(2)}) collective-permute-start(f32[32,128]{1,0:T(8,128)S(1)} %slice_add_fusion), channel_id=1, source_target_pairs={{0,224},{32,64},{64,32},{96,128},{128,96},{160,192},{192,160},{224... | collective-permute-start | bytes 49160 | tf_op jit(solution)/shard_map/ppermute | solution.py:438
  101.4 1.5 collective-permute-done.27
  104.2 3.5 %collective-permute-done.28 = f32[32,128]{1,0:T(8,128)S(1)} collective-permute-done((f32[32,128]{1,0:T(8,128)S(1)}, f32[32,128]{1,0:T(8,128)S(1)}, u32[]{:S(2)}, u32[]{:S(2)}) %collective-permute-start.28) | collective-permute-done | bytes 16416 | tf_op jit(solution)/shard_map/ppermute | solution.py:438
  107.7 7.8 %all-gather.2.cloned.1.call-done.pack = f32[512,10880]{1,0:T(8,128)} async-done(((f32[16,10880]{1,0:T(8,128)}), f32[512,10880]{1,0:T(8,128)}) %all-gather.2.cloned.1.call-update) | async-done | bytes 22282256 | tf_op jit(solution)/shard_map/all_gather | solution.py:474
  115.6 3.7 %shard_map.52 = f32[32,128]{1,0:T(8,128)S(1)} custom-call(f32[512,10880]{1,0:T(8,128)} %all-gather.2.cloned.1.call-done.pack, f32[32,128]{1,0:T(8,128)S(1)} %add.100.summed), custom_call_target="tpu_custom_call" | custom-call | flops 536870912 | bytes 1048576 | tf_op jit(solution)/shard_map/pallas_call | solution.py:421
  119.3 1.4 collective-permute-start.29
  121.9 3.0 %collective-permute-start.30 = (f32[32,128]{1,0:T(8,128)S(1)}, f32[32,128]{1,0:T(8,128)S(1)}, u32[]{:S(2)}, u32[]{:S(2)}) collective-permute-start(f32[32,128]{1,0:T(8,128)S(1)} %add.101), channel_id=1, source_target_pairs={{0,224},{32,64},{64,32},{96,128},{128,96},{160,192},{192,160},{224... | collective-permute-start | bytes 49160 | tf_op jit(solution)/shard_map/ppermute | solution.py:438
  126.1 2.9 %collective-permute-start.31 = (f32[32,128]{1,0:T(8,128)S(1)}, f32[32,128]{1,0:T(8,128)S(1)}, u32[]{:S(2)}, u32[]{:S(2)}) collective-permute-start(f32[32,128]{1,0:T(8,128)S(1)} %add.102), channel_id=1, source_target_pairs={{0,96},{32,192},{64,160},{96,0},{128,224},{160,64},{192,32},{224,1... | collective-permute-start | bytes 49160 | tf_op jit(solution)/shard_map/ppermute | solution.py:438
  129.0 1.5 collective-permute-done.31
  130.5 3.5 %shard_map.53 = f32[16,128]{1,0:T(8,128)S(1)} custom-call(f32[512,10880]{1,0:T(8,128)} %all-gather.2.cloned.1.call-done.pack, f32[16,128]{1,0:T(8,128)S(1)} %get-tuple-element.49.residual, f32[32,128]{1,0:T(8,128)S(1)} %add.103.rest_0_.s5), custom_call_target="tpu_custom_call" | custom-call | flops 536870912 | bytes 1048576 | tf_op jit(solution)/shard_map/pallas_call | solution.py:421
  135.0 1.6 collective-permute-done.32
  136.6 1.9 %collective-permute-start.33 = (f32[16,128]{1,0:T(8,128)S(1)}, f32[16,128]{1,0:T(8,128)S(1)}, u32[]{:S(2)}, u32[]{:S(2)}) collective-permute-start(f32[16,128]{1,0:T(8,128)S(1)} %add.104), channel_id=1, source_target_pairs={{0,64},{32,96},{64,0},{96,32},{128,192},{160,224},{192,128},{224,1... | collective-permute-start | bytes 24584 | tf_op jit(solution)/shard_map/ppermute | solution.py:438
  138.5 1.4 collective-permute-done.33
  140.0 2.9 %shard_map.54 = f32[8,128]{1,0:T(8,128)S(1)} custom-call(f32[512,10880]{1,0:T(8,128)} %all-gather.2.cloned.1.call-done.pack, f32[8,128]{1,0:T(8,128)S(1)} %get-tuple-element.50.residual, f32[32,128]{1,0:T(8,128)S(1)} %add.103.rest_0_.s5, f32[16,128]{1,0:T(8,128)S(1)} %add.105.rest_1_.s4), custom_call_target="tpu_custom_call" | custom-call | flops 536870912 | bytes 1048576 | tf_op jit(solution)/shard_map/pallas_call | solution.py:421
  143.9 1.4 collective-permute-done.34
  145.4 6.0 %shard_map.55 = f32[16,128]{1,0:T(8,128)S(1)} custom-call(f32[512,10880]{1,0:T(8,128)} %all-gather.2.cloned.1.call-done.pack, f32[8,128]{1,0:T(8,128)S(1)} %slice.30.r01, f32[4,128]{1,0:T(4,128)S(1)} %get-tuple-element.48.r2, f32[32,128]{1,0:T(8,128)S(1)} %add.103.rest_0_.s5, f32[16,128]{1,0:T(8,128)S(1)} %add.105.rest_1_.s4, f32[8,128]{1,0:T(8,128)S(1)} %add.106.s3), custom_call_target="tpu_custom_call" | custom-call | flops 536870912 | bytes 1048576 | tf_op jit(solution)/shard_map/pallas_call | solution.py:421
  151.9 21.4 %all_to_all.5 = f32[32,6,16]{2,1,0:T(8,128)S(1)} all-to-all(f32[32,6,16]{2,1,0:T(8,128)S(1)} %copy.8), channel_id=1, replica_groups=mesh['z'=8,'x'=4,'blk'=8] {'x','blk'}, dimensions={0} | all-to-all | bytes 24576 | tf_op jit(solution)/shard_map/all_to_all | solution.py:556
  (90 shorter events, 24.2 us)
Async XLA Ops:
  6.5 109.0 %all-gather.2.cloned.1.call-start = ((), (), s32[]{:S(2)}) async-start(), calls=%async_computation.1 | async-start | bytes 22978560 | tf_op jit(solution)/shard_map/all_gather | solution.py:474
  9.8 7.6 %collective-permute-start = (f32[16,2944]{1,0:T(8,128)}, f32[16,2944]{1,0:T(8,128)S(1)}, u32[]{:S(2)}, u32[]{:S(2)}) collective-permute-start(f32[16,2944]{1,0:T(8,128)} %get-tuple-element.30.refs_0_), channel_id=1, source_target_pairs={{0,4},{1,5},{2,6},{3,7},{4,0},{5,1},{6,2},{7,3},{8,12},{9,13},{10,... | collective-permute-start | bytes 565256 | tf_op jit(solution)/shard_map/ppermute | solution.py:438
  13.7 9.3 %collective-permute-start.5 = (f32[16,2944]{1,0:T(8,128)}, f32[16,2944]{1,0:T(8,128)S(1)}, u32[]{:S(2)}, u32[]{:S(2)}) collective-permute-start(f32[16,2944]{1,0:T(8,128)} %get-tuple-element.30.refs_0_), channel_id=1, source_target_pairs={{0,2},{1,3},{2,4},{3,5},{4,6},{5,7},{6,0},{7,1},{8,10},{9,11},{10,... | collective-permute-start | bytes 565256 | tf_op jit(solution)/shard_map/ppermute | solution.py:438
  14.1 10.2 %collective-permute-start.6 = (f32[16,2944]{1,0:T(8,128)}, f32[16,2944]{1,0:T(8,128)S(1)}, u32[]{:S(2)}, u32[]{:S(2)}) collective-permute-start(f32[16,2944]{1,0:T(8,128)} %get-tuple-element.30.refs_0_), channel_id=1, source_target_pairs={{0,6},{1,7},{2,0},{3,1},{4,2},{5,3},{6,4},{7,5},{8,14},{9,15},{10,... | collective-permute-start | bytes 565256 | tf_op jit(solution)/shard_map/ppermute | solution.py:438
  17.5 6.8 %collective-permute-start.1 = (f32[16,2944]{1,0:T(8,128)S(1)}, f32[16,2944]{1,0:T(8,128)S(1)}, u32[]{:S(2)}, u32[]{:S(2)}) collective-permute-start(f32[16,2944]{1,0:T(8,128)S(1)} %collective-permute-done.refs_3_), channel_id=1, source_target_pairs={{0,1},{1,0},{2,3},{3,2},{4,5},{5,4},{6,7},{7,6},{8,9},{9,8},{10,11... | collective-permute-start | bytes 565256 | tf_op jit(solution)/shard_map/ppermute | solution.py:438
  21.7 5.3 %collective-permute-start.7 = (f32[16,2944]{1,0:T(8,128)}, f32[16,2944]{1,0:T(8,128)S(1)}, u32[]{:S(2)}, u32[]{:S(2)}) collective-permute-start(f32[16,2944]{1,0:T(8,128)} %get-tuple-element.30.refs_0_), channel_id=1, source_target_pairs={{0,1},{1,0},{2,3},{3,2},{4,5},{5,4},{6,7},{7,6},{8,9},{9,8},{10,11... | collective-permute-start | bytes 565256 | tf_op jit(solution)/shard_map/ppermute | solution.py:438
  22.9 4.7 %collective-permute-start.8 = (f32[16,2944]{1,0:T(8,128)S(1)}, f32[16,2944]{1,0:T(8,128)S(1)}, u32[]{:S(2)}, u32[]{:S(2)}) collective-permute-start(f32[16,2944]{1,0:T(8,128)S(1)} %collective-permute-done.5.refs_1_), channel_id=1, source_target_pairs={{0,1},{1,0},{2,3},{3,2},{4,5},{5,4},{6,7},{7,6},{8,9},{9,8},{10,11... | collective-permute-start | bytes 565256 | tf_op jit(solution)/shard_map/ppermute | solution.py:438
  24.3 3.4 %collective-permute-start.9 = (f32[16,2944]{1,0:T(8,128)S(1)}, f32[16,2944]{1,0:T(8,128)S(1)}, u32[]{:S(2)}, u32[]{:S(2)}) collective-permute-start(f32[16,2944]{1,0:T(8,128)S(1)} %collective-permute-done.6.refs_2_), channel_id=1, source_target_pairs={{0,1},{1,0},{2,3},{3,2},{4,5},{5,4},{6,7},{7,6},{8,9},{9,8},{10,11... | collective-permute-start | bytes 565256 | tf_op jit(solution)/shard_map/ppermute | solution.py:438
  24.3 22.5 %collective-permute-start.2 = (f32[16,4096]{1,0:T(8,128)}, f32[16,4096]{1,0:T(8,128)S(1)}, u32[]{:S(2)}, u32[]{:S(2)}) collective-permute-start(f32[16,4096]{1,0:T(8,128)} %get-tuple-element.38.refs_0_), channel_id=1, source_target_pairs={{0,2},{1,3},{2,4},{3,5},{4,6},{5,7},{6,0},{7,1},{8,10},{9,11},{10,... | collective-permute-start | bytes 786440 | tf_op jit(solution)/shard_map/ppermute | solution.py:438
  25.2 21.6 %collective-permute-start.3 = (f32[16,4096]{1,0:T(8,128)}, f32[16,4096]{1,0:T(8,128)S(1)}, u32[]{:S(2)}, u32[]{:S(2)}) collective-permute-start(f32[16,4096]{1,0:T(8,128)} %get-tuple-element.38.refs_0_), channel_id=1, source_target_pairs={{0,6},{1,7},{2,0},{3,1},{4,2},{5,3},{6,4},{7,5},{8,14},{9,15},{10,... | collective-permute-start | bytes 786440 | tf_op jit(solution)/shard_map/ppermute | solution.py:438
  27.0 21.3 %collective-permute-start.4 = (f32[16,4096]{1,0:T(8,128)}, f32[16,4096]{1,0:T(8,128)S(1)}, u32[]{:S(2)}, u32[]{:S(2)}) collective-permute-start(f32[16,4096]{1,0:T(8,128)} %get-tuple-element.38.refs_0_), channel_id=1, source_target_pairs={{0,4},{1,5},{2,6},{3,7},{4,0},{5,1},{6,2},{7,3},{8,12},{9,13},{10,... | collective-permute-start | bytes 786440 | tf_op jit(solution)/shard_map/ppermute | solution.py:438
  27.7 1.0 copy-start.2
  31.4 2.9 %collective-permute-start.10 = (f32[8,128]{1,0:T(8,128)S(1)}, f32[8,128]{1,0:T(8,128)S(1)}, u32[]{:S(2)}, u32[]{:S(2)}) collective-permute-start(f32[8,128]{1,0:T(8,128)S(1)} %get-tuple-element.33), channel_id=1, source_target_pairs={{0,8},{8,0},{16,24},{24,16},{1,9},{9,1},{17,25},{25,17},{2,10},{10... | collective-permute-start | bytes 12296 | tf_op jit(solution)/shard_map/ppermute | solution.py:438
  34.4 0.9 copy-start.3
  36.9 3.0 %collective-permute-start.11 = (f32[16,128]{1,0:T(8,128)S(1)}, f32[16,128]{1,0:T(8,128)S(1)}, u32[]{:S(2)}, u32[]{:S(2)}) collective-permute-start(f32[16,128]{1,0:T(8,128)S(1)} %get-tuple-element.35), channel_id=1, source_target_pairs={{0,8},{8,0},{16,24},{24,16},{1,9},{9,1},{17,25},{25,17},{2,10},{10... | collective-permute-start | bytes 24584 | tf_op jit(solution)/shard_map/ppermute | solution.py:438
  39.9 4.2 %collective-permute-start.12 = (f32[16,128]{1,0:T(8,128)S(1)}, f32[16,128]{1,0:T(8,128)S(1)}, u32[]{:S(2)}, u32[]{:S(2)}) collective-permute-start(f32[16,128]{1,0:T(8,128)S(1)} %add.87), channel_id=1, source_target_pairs={{0,24},{8,16},{16,8},{24,0},{1,25},{9,17},{17,9},{25,1},{2,26},{10... | collective-permute-start | bytes 24584 | tf_op jit(solution)/shard_map/ppermute | solution.py:438
  44.1 0.9 copy-start.4
  48.3 11.7 %collective-permute-start.13 = (f32[16,4096]{1,0:T(8,128)}, f32[16,4096]{1,0:T(8,128)S(1)}, u32[]{:S(2)}, u32[]{:S(2)}) collective-permute-start(f32[16,4096]{1,0:T(8,128)} %get-tuple-element.38.refs_0_), channel_id=1, source_target_pairs={{0,1},{1,0},{2,3},{3,2},{4,5},{5,4},{6,7},{7,6},{8,9},{9,8},{10,11... | collective-permute-start | bytes 786440 | tf_op jit(solution)/shard_map/ppermute | solution.py:438
  50.2 9.8 %collective-permute-start.14 = (f32[16,4096]{1,0:T(8,128)S(1)}, f32[16,4096]{1,0:T(8,128)S(1)}, u32[]{:S(2)}, u32[]{:S(2)}) collective-permute-start(f32[16,4096]{1,0:T(8,128)S(1)} %collective-permute-done.2.refs_1_), channel_id=1, source_target_pairs={{0,1},{1,0},{2,3},{3,2},{4,5},{5,4},{6,7},{7,6},{8,9},{9,8},{10,11... | collective-permute-start | bytes 786440 | tf_op jit(solution)/shard_map/ppermute | solution.py:438
  50.3 9.7 %collective-permute-start.15 = (f32[16,4096]{1,0:T(8,128)S(1)}, f32[16,4096]{1,0:T(8,128)S(1)}, u32[]{:S(2)}, u32[]{:S(2)}) collective-permute-start(f32[16,4096]{1,0:T(8,128)S(1)} %collective-permute-done.3.refs_2_), channel_id=1, source_target_pairs={{0,1},{1,0},{2,3},{3,2},{4,5},{5,4},{6,7},{7,6},{8,9},{9,8},{10,11... | collective-permute-start | bytes 786440 | tf_op jit(solution)/shard_map/ppermute | solution.py:438
  50.7 9.3 %collective-permute-start.16 = (f32[16,4096]{1,0:T(8,128)S(1)}, f32[16,4096]{1,0:T(8,128)S(1)}, u32[]{:S(2)}, u32[]{:S(2)}) collective-permute-start(f32[16,4096]{1,0:T(8,128)S(1)} %collective-permute-done.4.refs_3_), channel_id=1, source_target_pairs={{0,1},{1,0},{2,3},{3,2},{4,5},{5,4},{6,7},{7,6},{8,9},{9,8},{10,11... | collective-permute-start | bytes 786440 | tf_op jit(solution)/shard_map/ppermute | solution.py:438
  50.8 2.6 %collective-permute-start.17 = (f32[32,128]{1,0:T(8,128)S(1)}, f32[32,128]{1,0:T(8,128)S(1)}, u32[]{:S(2)}, u32[]{:S(2)}) collective-permute-start(f32[32,128]{1,0:T(8,128)S(1)} %get-tuple-element.37), channel_id=1, source_target_pairs={{0,8},{8,0},{16,24},{24,16},{1,9},{9,1},{17,25},{25,17},{2,10},{10... | collective-permute-start | bytes 49160 | tf_op jit(solution)/shard_map/ppermute | solution.py:438
  53.4 3.8 %collective-permute-start.18 = (f32[32,128]{1,0:T(8,128)S(1)}, f32[32,128]{1,0:T(8,128)S(1)}, u32[]{:S(2)}, u32[]{:S(2)}) collective-permute-start(f32[32,128]{1,0:T(8,128)S(1)} %add.89), channel_id=1, source_target_pairs={{0,24},{8,16},{16,8},{24,0},{1,25},{9,17},{17,9},{25,1},{2,26},{10... | collective-permute-start | bytes 49160 | tf_op jit(solution)/shard_map/ppermute | solution.py:438
  57.2 2.8 %collective-permute-start.19 = (f32[32,128]{1,0:T(8,128)S(1)}, f32[32,128]{1,0:T(8,128)S(1)}, u32[]{:S(2)}, u32[]{:S(2)}) collective-permute-start(f32[32,128]{1,0:T(8,128)S(1)} %add.90), channel_id=1, source_target_pairs={{0,32},{32,0},{64,96},{96,64},{128,160},{160,128},{192,224},{224,1... | collective-permute-start | bytes 49160 | tf_op jit(solution)/shard_map/ppermute | solution.py:438
  60.0 1.0 copy-start
  62.9 3.0 %collective-permute-start.20 = (f32[64,128]{1,0:T(8,128)S(1)}, f32[64,128]{1,0:T(8,128)S(1)}, u32[]{:S(2)}, u32[]{:S(2)}) collective-permute-start(f32[64,128]{1,0:T(8,128)S(1)} %get-tuple-element.44), channel_id=1, source_target_pairs={{0,8},{8,0},{16,24},{24,16},{1,9},{9,1},{17,25},{25,17},{2,10},{10... | collective-permute-start | bytes 98312 | tf_op jit(solution)/shard_map/ppermute | solution.py:438
  65.9 5.5 %collective-permute-start.21 = (f32[64,128]{1,0:T(8,128)S(1)}, f32[64,128]{1,0:T(8,128)S(1)}, u32[]{:S(2)}, u32[]{:S(2)}) collective-permute-start(f32[64,128]{1,0:T(8,128)S(1)} %add.92), channel_id=1, source_target_pairs={{0,24},{8,16},{16,8},{24,0},{1,25},{9,17},{17,9},{25,1},{2,26},{10... | collective-permute-start | bytes 98312 | tf_op jit(solution)/shard_map/ppermute | solution.py:438
  71.4 3.6 %collective-permute-start.22 = (f32[64,128]{1,0:T(8,128)S(1)}, f32[64,128]{1,0:T(8,128)S(1)}, u32[]{:S(2)}, u32[]{:S(2)}) collective-permute-start(f32[64,128]{1,0:T(8,128)S(1)} %add.93), channel_id=1, source_target_pairs={{0,32},{32,0},{64,96},{96,64},{128,160},{160,128},{192,224},{224,1... | collective-permute-start | bytes 98312 | tf_op jit(solution)/shard_map/ppermute | solution.py:438
  75.0 5.4 %collective-permute-start.23 = (f32[64,128]{1,0:T(8,128)S(1)}, f32[64,128]{1,0:T(8,128)S(1)}, u32[]{:S(2)}, u32[]{:S(2)}) collective-permute-start(f32[64,128]{1,0:T(8,128)S(1)} %add.94), channel_id=1, source_target_pairs={{0,64},{32,96},{64,0},{96,32},{128,192},{160,224},{192,128},{224,1... | collective-permute-start | bytes 98312 | tf_op jit(solution)/shard_map/ppermute | solution.py:438
  80.4 1.0 copy-start.1
  83.8 5.4 %collective-permute-start.24 = (f32[2,40,128]{2,1,0:T(8,128)S(1)}, f32[2,40,128]{2,1,0:T(8,128)S(1)}, u32[]{:S(2)}, u32[]{:S(2)}) collective-permute-start(f32[2,40,128]{2,1,0:T(8,128)S(1)} %get-tuple-element.47), channel_id=1, source_target_pairs={{0,24},{8,16},{16,8},{24,0},{1,25},{9,17},{17,9},{25,1},{2,26},{10... | collective-permute-start | bytes 122888 | tf_op jit(solution)/shard_map/ppermute | solution.py:438
  89.3 3.5 %collective-permute-start.25 = (f32[40,128]{1,0:T(8,128)S(1)}, f32[40,128]{1,0:T(8,128)S(1)}, u32[]{:S(2)}, u32[]{:S(2)}) collective-permute-start(f32[40,128]{1,0:T(8,128)S(1)} %slice_bitcast_fusion), channel_id=1, source_target_pairs={{0,8},{8,0},{16,24},{24,16},{1,9},{9,1},{17,25},{25,17},{2,10},{10... | collective-permute-start | bytes 61448 | tf_op jit(solution)/shard_map/ppermute | solution.py:438
  92.8 3.1 %collective-permute-start.26 = (f32[32,128]{1,0:T(8,128)S(1)}, f32[32,128]{1,0:T(8,128)S(1)}, u32[]{:S(2)}, u32[]{:S(2)}) collective-permute-start(f32[32,128]{1,0:T(8,128)S(1)} %slice.31), channel_id=1, source_target_pairs={{0,32},{32,0},{64,96},{96,64},{128,160},{160,128},{192,224},{224,1... | collective-permute-start | bytes 49160 | tf_op jit(solution)/shard_map/ppermute | solution.py:438
  95.9 7.1 %collective-permute-start.27 = (f32[32,128]{1,0:T(8,128)S(1)}, f32[32,128]{1,0:T(8,128)S(1)}, u32[]{:S(2)}, u32[]{:S(2)}) collective-permute-start(f32[32,128]{1,0:T(8,128)S(1)} %slice_add_fusion), channel_id=1, source_target_pairs={{0,224},{32,64},{64,32},{96,128},{128,96},{160,192},{192,160},{224... | collective-permute-start | bytes 49160 | tf_op jit(solution)/shard_map/ppermute | solution.py:438
  103.0 4.8 %collective-permute-start.28 = (f32[32,128]{1,0:T(8,128)S(1)}, f32[32,128]{1,0:T(8,128)S(1)}, u32[]{:S(2)}, u32[]{:S(2)}) collective-permute-start(f32[32,128]{1,0:T(8,128)S(1)} %add.99), channel_id=1, source_target_pairs={{0,96},{32,192},{64,160},{96,0},{128,224},{160,64},{192,32},{224,1... | collective-permute-start | bytes 49160 | tf_op jit(solution)/shard_map/ppermute | solution.py:438
  119.3 2.7 %collective-permute-start.29 = (f32[32,128]{1,0:T(8,128)S(1)}, f32[32,128]{1,0:T(8,128)S(1)}, u32[]{:S(2)}, u32[]{:S(2)}) collective-permute-start(f32[32,128]{1,0:T(8,128)S(1)} %shard_map.52), channel_id=1, source_target_pairs={{0,32},{32,0},{64,96},{96,64},{128,160},{160,128},{192,224},{224,1... | collective-permute-start | bytes 49160 | tf_op jit(solution)/shard_map/ppermute | solution.py:438
  121.9 4.2 %collective-permute-start.30 = (f32[32,128]{1,0:T(8,128)S(1)}, f32[32,128]{1,0:T(8,128)S(1)}, u32[]{:S(2)}, u32[]{:S(2)}) collective-permute-start(f32[32,128]{1,0:T(8,128)S(1)} %add.101), channel_id=1, source_target_pairs={{0,224},{32,64},{64,32},{96,128},{128,96},{160,192},{192,160},{224... | collective-permute-start | bytes 49160 | tf_op jit(solution)/shard_map/ppermute | solution.py:438
  126.1 4.4 %collective-permute-start.31 = (f32[32,128]{1,0:T(8,128)S(1)}, f32[32,128]{1,0:T(8,128)S(1)}, u32[]{:S(2)}, u32[]{:S(2)}) collective-permute-start(f32[32,128]{1,0:T(8,128)S(1)} %add.102), channel_id=1, source_target_pairs={{0,96},{32,192},{64,160},{96,0},{128,224},{160,64},{192,32},{224,1... | collective-permute-start | bytes 49160 | tf_op jit(solution)/shard_map/ppermute | solution.py:438
  134.0 2.6 %collective-permute-start.32 = (f32[16,128]{1,0:T(8,128)S(1)}, f32[16,128]{1,0:T(8,128)S(1)}, u32[]{:S(2)}, u32[]{:S(2)}) collective-permute-start(f32[16,128]{1,0:T(8,128)S(1)} %shard_map.53), channel_id=1, source_target_pairs={{0,32},{32,0},{64,96},{96,64},{128,160},{160,128},{192,224},{224,1... | collective-permute-start | bytes 24584 | tf_op jit(solution)/shard_map/ppermute | solution.py:438
  136.6 3.4 %collective-permute-start.33 = (f32[16,128]{1,0:T(8,128)S(1)}, f32[16,128]{1,0:T(8,128)S(1)}, u32[]{:S(2)}, u32[]{:S(2)}) collective-permute-start(f32[16,128]{1,0:T(8,128)S(1)} %add.104), channel_id=1, source_target_pairs={{0,64},{32,96},{64,0},{96,32},{128,192},{160,224},{192,128},{224,1... | collective-permute-start | bytes 24584 | tf_op jit(solution)/shard_map/ppermute | solution.py:438
  142.8 2.5 %collective-permute-start.34 = (f32[8,128]{1,0:T(8,128)S(1)}, f32[8,128]{1,0:T(8,128)S(1)}, u32[]{:S(2)}, u32[]{:S(2)}) collective-permute-start(f32[8,128]{1,0:T(8,128)S(1)} %shard_map.54), channel_id=1, source_target_pairs={{0,32},{32,0},{64,96},{96,64},{128,160},{160,128},{192,224},{224,1... | collective-permute-start | bytes 12296 | tf_op jit(solution)/shard_map/ppermute | solution.py:438
Sparse Core Ops, SparseCore 0:
  10.0 105.5 all-gather.1
